TPU v7x, 128 devices: a whole 4x4x4 slice. The times are simulated.
128 devices in a mesh: chan: 16 (over z, y_lo, core), tm: 8 (over x, y_hi).
Axes of the slice: x: 4, y: 4 (y_hi: 2, y_lo: 2; y = y_hi * 2 + y_lo), z: 4, core: 2. Of those that a mesh axis runs over, the one named last changes fastest.
Arguments:
- traces: bfloat16 [2048, 256, 512], P('chan', 'tm'), may hold values from -34 to 34
- pairing: int32 [3, 16], replicated, may hold values from 0 to 15, as said below
Outputs:
- correlations: float32 [3, 64, 2048, 128], P(None, 'tm', 'chan')
Inputs may be any that keep to these rules, and one draw needn't show every extreme that they name: Each row pairs every block with another block, both ways (pairing[r, pairing[r, c]] = c, never c itself); the rows are distinct rounds of one round-robin tournament, so no two blocks meet twice.
All inputs are finite; a program needn't handle non-finite values.
Results may differ from a plain program's by a relative error of at most 0.0068.
Values may be sent and summed in bfloat16 or wider, within the bound.
No kernel may reach another device: no remote copies, remote signals or barrier semaphores. Data moves between devices by JAX's collectives and lax.ppermute only.
A program may use at most 128 MiB of HBM per device.

v0:
```python
import functools
import math

import jax
import jax.numpy as jnp
import numpy as np
from jax import lax
from jax.experimental import pallas as pl
from jax.experimental.pallas import tpu as pltpu
from jax.sharding import PartitionSpec as P

FREQS = 256
SAMPLES = 512
LAGS = 64
CH = 128
WIN = 32
GROUPS = 64
ROWS = 256
N_CHAN = 16
N_TM = 8
WATER = 1.0
EPS = 1e-06
F32 = jnp.float32
BF16 = jnp.bfloat16


def forward_rows():
    freq = np.arange(FREQS)[:, None]
    sample = np.arange(SAMPLES)[None, :]
    phase = (freq * sample % SAMPLES) * (2.0 * math.pi / SAMPLES)
    both = np.stack([np.cos(phase), -np.sin(phase)], 0)
    both = both.reshape(2, GROUPS, 4, SAMPLES).transpose(1, 0, 2, 3)
    return both.reshape(2 * FREQS, SAMPLES).astype(np.float32).astype(BF16)


def lag_rows():
    lag = np.arange(LAGS)[:, None]
    freq = np.arange(FREQS)[None, :]
    phase = (lag * freq % SAMPLES) * (2.0 * math.pi / SAMPLES)
    both = np.stack([np.cos(phase), -np.sin(phase)], 0)
    both = both.reshape(2, N_TM, 1, 8, GROUPS, 1, 4)
    parity = np.eye(2).reshape(1, 1, 2, 1, 1, 2, 1)
    return (both * parity).reshape(2, 2 * LAGS, 2 * FREQS).astype(np.float32).astype(BF16)


def taper_row():
    pos = np.arange(SAMPLES)
    taper = 0.5 - 0.5 * np.cos((pos + 0.5) * (2.0 * math.pi / SAMPLES))
    return taper.astype(np.float32).reshape(1, SAMPLES)


CHUNK = 16
PART = 4


def whiten_kernel(
    traces, taper_hbm, table_hbm, out, raw, taper, table, tapered, white_rows, small_sems, in_sems, out_sems
):
    taper_copy = pltpu.make_async_copy(taper_hbm, taper, small_sems.at[0])
    table_copy = pltpu.make_async_copy(table_hbm, table, small_sems.at[1])

    def arrival(chunk):
        rows = pl.ds(chunk * CHUNK, CHUNK)
        return pltpu.make_async_copy(traces.at[rows], raw.at[rows], in_sems.at[chunk])

    def departure(part):
        rows = pl.ds(pl.multiple_of(part * PART * 16, PART * 16), PART * 16)
        return pltpu.make_async_copy(
            white_rows.at[:, rows, :], out.at[:, rows, :], out_sems.at[part]
        )

    taper_copy.start()
    for chunk in range(CH // CHUNK):
        arrival(chunk).start()
    table_copy.start()
    taper_copy.wait()

    def taper_step(chunk, carry):
        arrival(chunk).wait()
        for half in range(CHUNK // 8):
            first = chunk * CHUNK + half * 8
            rows = raw[pl.ds(first, 8)].astype(F32)
            rows = rows - jnp.mean(rows, axis=2, keepdims=True)
            rows = (rows * taper[...].reshape(1, 1, SAMPLES)).reshape(8 * WIN, SAMPLES)
            for tile in range(4):
                tapered[tile, pl.ds(first * WIN, 8 * WIN), :] = rows[:, tile * 128 : tile * 128 + 128]
        return carry

    lax.fori_loop(0, CH // CHUNK, taper_step, 0)
    table_copy.wait()

    def window_pairs(part, carry):
        for pair in [part * PART + inner for inner in range(PART)]:
            columns = []
            for half in range(2):
                tiles = [
                    tapered[tile, pl.ds(pair * 2 + half, CH, stride=WIN), :] for tile in range(4)
                ]
                columns.append(jnp.concatenate(tiles, axis=1).astype(BF16))
            columns = jnp.concatenate(columns, axis=0)
            spec = lax.dot_general(
                table[...], columns, (((1,), (1,)), ((), ())), preferred_element_type=F32
            ).reshape(GROUPS, 8, 2 * CH)
            square = spec * spec
            level = jnp.sum(jnp.sum(square, axis=0), axis=0, keepdims=True) * (1.0 / FREQS)
            power = square + pltpu.roll(square, 4, 1)
            white = spec * lax.rsqrt(power + (WATER * level + EPS).reshape(1, 1, 2 * CH))
            white = jnp.concatenate([white[:, :, :CH], white[:, :, CH:]], axis=1)
            white_rows[:, pl.ds(pl.multiple_of(pair * 16, 16), 16), :] = white.astype(BF16)
        departure(part).start()
        return carry

    lax.fori_loop(0, WIN // 2 // PART, window_pairs, 0)
    for part in range(WIN // 2 // PART):
        departure(part).wait()


def whiten(traces):
    return pl.pallas_call(
        whiten_kernel,
        out_shape=jax.ShapeDtypeStruct((GROUPS, ROWS, CH), BF16),
        in_specs=[pl.BlockSpec(memory_space=pl.ANY)] * 3,
        out_specs=pl.BlockSpec(memory_space=pl.ANY),
        scratch_shapes=[
            pltpu.VMEM((CH, WIN, SAMPLES), BF16),
            pltpu.VMEM((1, SAMPLES), F32),
            pltpu.VMEM((2 * FREQS, SAMPLES), BF16),
            pltpu.VMEM((4, CH * WIN, 128), F32),
            pltpu.VMEM((GROUPS, ROWS, CH), BF16),
            pltpu.SemaphoreType.DMA((2,)),
            pltpu.SemaphoreType.DMA((CH // CHUNK,)),
            pltpu.SemaphoreType.DMA((WIN // 2 // PART,)),
        ],
        compiler_params=pltpu.CompilerParams(vmem_limit_bytes=60 * 2**20),
        cost_estimate=pl.CostEstimate(flops=2 * 2**30, bytes_accessed=2**23, transcendentals=2**20),
        name="whiten",
    )(traces, jnp.asarray(taper_row()), jnp.asarray(forward_rows()))


def expand_kernel(spec, out, wide):
    lane = lax.broadcasted_iota(jnp.int32, (CH, ROWS), 1)
    for part in range(spec.shape[0]):
        turned = spec[part].astype(F32).T
        for f in range(4):
            kept = jnp.where(lane % 4 == f, turned, 0.0)
            for tile in range(2):
                wide[tile, pl.ds(f, CH, stride=4), :] = kept[:, tile * 128 : tile * 128 + 128]
        for tile in range(2):
            out[part, :, tile * 128 : tile * 128 + 128] = wide[tile].astype(BF16)


def expand(spec):
    per = 4
    return pl.pallas_call(
        expand_kernel,
        grid=(GROUPS // per,),
        out_shape=jax.ShapeDtypeStruct((GROUPS, 4 * CH, ROWS), BF16),
        in_specs=[pl.BlockSpec((per, ROWS, CH), lambda g: (g, 0, 0))],
        out_specs=pl.BlockSpec((per, 4 * CH, ROWS), lambda g: (g, 0, 0)),
        scratch_shapes=[pltpu.VMEM((2, 4 * CH, 128), F32)],
        compiler_params=pltpu.CompilerParams(vmem_limit_bytes=32 * 2**20),
        cost_estimate=pl.CostEstimate(flops=2**26, bytes_accessed=20 * 2**20, transcendentals=0),
        name="expand",
    )(spec)


def correlate_kernel(steps, own_hbm, partner_hbm, table, *refs):
    outs = refs[:4]
    own, partner, cross, own_sems, partner_sems = refs[4:]
    step = pl.program_id(0)
    per = GROUPS // steps
    sub = lax.broadcasted_iota(jnp.int32, (WIN, 8, CH), 1)

    def arrivals(chunk):
        groups = pl.ds(chunk * per, per)
        return (
            pltpu.make_async_copy(own_hbm.at[groups], own.at[groups], own_sems.at[chunk]),
            pltpu.make_async_copy(
                partner_hbm.at[groups], partner.at[groups], partner_sems.at[chunk]
            ),
        )

    @pl.when(step == 0)
    def _():
        for chunk in range(steps):
            for copy in arrivals(chunk):
                copy.start()

    @pl.when(step < steps)
    def _():
        for copy in arrivals(step):
            copy.wait()
        for pair in range(per // 2):
            halves = []
            for half in range(2):
                group = step * per + 2 * pair + half
                part = partner[group]
                wide = part.astype(F32).reshape(WIN, 8, CH)
                turned = jnp.where(sub < 4, -1.0, 1.0) * pltpu.roll(wide, 4, 1)
                right = jnp.concatenate([part, turned.reshape(ROWS, CH).astype(BF16)], axis=1)
                prod = jnp.dot(own[group], right, preferred_element_type=F32)
                halves.append(prod.reshape(CH // 2, 8, 2 * CH))
            rows = jnp.concatenate(halves, axis=1).astype(BF16)
            first = pl.multiple_of((step * (per // 2) + pair) * 16, 16)
            cross[:, pl.ds(first, 16), :] = rows

    @pl.when(step >= steps)
    def _():
        scale = 1.0 / math.sqrt(FREQS * WIN * N_TM)
        signs, chunk = outs[0].shape[1:3]
        base = (step - steps) * chunk

        def channel_pairs(idx, carry):
            first, second = cross[base + 2 * idx], cross[base + 2 * idx + 1]
            even = jnp.concatenate([first[:, :CH], second[:, :CH]], axis=1)
            odd = jnp.concatenate([first[:, CH:], second[:, CH:]], axis=1)
            even = jnp.dot(table[0], even, preferred_element_type=F32)
            odd = jnp.dot(table[1], odd, preferred_element_type=F32)
            for sign in range(signs):
                value = (even - odd if sign else even + odd) * scale
                value = value.astype(BF16).reshape(4, 2, 16, 2 * CH)
                for shift in range(4):
                    outs[shift][:, sign, 2 * idx] = value[shift, :, :, :CH]
                    outs[shift][:, sign, 2 * idx + 1] = value[shift, :, :, CH:]
            return carry

        lax.fori_loop(0, chunk // 2, channel_pairs, 0, unroll=8)


def correlate(own, partner, table, signs):
    per, chunk = 8, 16
    steps, late = GROUPS // per, CH // 2 // chunk
    block = pl.BlockSpec(
        (2, signs, chunk, 16, CH), lambda g: (0, 0, jnp.maximum(g - steps, 0), 0, 0)
    )
    return pl.pallas_call(
        functools.partial(correlate_kernel, steps),
        grid=(steps + late,),
        out_shape=[jax.ShapeDtypeStruct((2, signs, CH // 2, 16, CH), BF16)] * 4,
        in_specs=[
            pl.BlockSpec(memory_space=pl.ANY),
            pl.BlockSpec(memory_space=pl.ANY),
            pl.BlockSpec((2, 2 * LAGS, 2 * FREQS), lambda g: (0, 0, 0)),
        ],
        out_specs=[block] * 4,
        scratch_shapes=[
            pltpu.VMEM((GROUPS, 4 * CH, ROWS), BF16),
            pltpu.VMEM((GROUPS, ROWS, CH), BF16),
            pltpu.VMEM((CH // 2, 2 * FREQS, 2 * CH), BF16),
            pltpu.SemaphoreType.DMA((steps,)),
            pltpu.SemaphoreType.DMA((steps,)),
        ],
        compiler_params=pltpu.CompilerParams(vmem_limit_bytes=56 * 2**20),
        cost_estimate=pl.CostEstimate(flops=2**34, bytes_accessed=24 * 2**20, transcendentals=0),
        name="correlate_both" if signs == 2 else "correlate_one",
    )(own, partner, table)


def pick_kernel(index, source, out, held, in_sems, out_sems):
    blocks = range(held.shape[0])
    into = [
        pltpu.make_async_copy(source.at[index[c]], held.at[c], in_sems.at[c]) for c in blocks
    ]
    away = [pltpu.make_async_copy(held.at[c], out.at[c], out_sems.at[c]) for c in blocks]
    for copy in into:
        copy.start()
    for arrive, leave in zip(into, away):
        arrive.wait()
        leave.start()
    for copy in away:
        copy.wait()


def pick(source, index):
    return pl.pallas_call(
        pick_kernel,
        grid_spec=pltpu.PrefetchScalarGridSpec(
            num_scalar_prefetch=1,
            grid=(1,),
            in_specs=[pl.BlockSpec(memory_space=pltpu.HBM)],
            out_specs=pl.BlockSpec(memory_space=pltpu.HBM),
            scratch_shapes=[
                pltpu.VMEM(source.shape, source.dtype),
                pltpu.SemaphoreType.DMA((source.shape[0],)),
                pltpu.SemaphoreType.DMA((source.shape[0],)),
            ],
        ),
        out_shape=jax.ShapeDtypeStruct(source.shape, source.dtype),
        compiler_params=pltpu.CompilerParams(vmem_limit_bytes=58 * 2**20),
        cost_estimate=pl.CostEstimate(
            flops=0, bytes_accessed=2 * source.size * source.dtype.itemsize, transcendentals=0
        ),
        name="pick",
    )(index, source)


def at(values, index):
    hit = index[:, None] == jnp.arange(N_CHAN, dtype=jnp.int32)[None, :]
    return jnp.sum(jnp.where(hit, values[None, :], 0), axis=1)


def orient(pairing):
    zero, one = pairing[0], pairing[1]
    hop = at(one, zero)
    least = jnp.arange(N_CHAN, dtype=jnp.int32)
    for _ in range(3):
        least = jnp.minimum(least, at(least, hop))
        hop = at(hop, hop)
    handles_zero = least < at(least, zero)
    return handles_zero, jnp.where(handles_zero, zero, one), jnp.where(handles_zero, one, zero)


def over_chan(blocks):
    return lax.all_to_all(blocks, "chan", split_axis=0, concat_axis=0, tiled=True)


def sent_over_x(parts):
    got = [parts[0]]
    for shift in (2, 1, 3):
        route = [(x * 2 + y, (x + shift) % 4 * 2 + y) for x in range(4) for y in range(2)]
        got.append(lax.ppermute(parts[shift], "tm", route))
    return got


def sum_of(blocks):
    total = blocks[0].astype(F32)
    for block in blocks[1:]:
        total = total + block.astype(F32)
    return total


def sum_over_y(halves):
    mine = lax.axis_index("tm") % 2
    other = lax.dynamic_index_in_dim(halves, 1 - mine, 0, keepdims=False).astype(BF16)
    other = lax.ppermute(other, "tm", [(t, t ^ 1) for t in range(N_TM)])
    return lax.dynamic_index_in_dim(halves, mine, 0, keepdims=False) + other.astype(F32)


def body(traces, pairing):
    spec = whiten(traces)
    spread = over_chan(spec.reshape(N_CHAN, GROUPS // N_CHAN * ROWS, CH))
    own = expand(spec)
    handles_zero, handled, other = orient(pairing)
    table = jnp.asarray(np.concatenate([lag_rows()] * 2, axis=1))
    table = lax.dynamic_slice_in_dim(table, lax.axis_index("tm") // 2 * 32, 2 * LAGS, 1)
    spread, own, handled, other, table = lax.optimization_barrier(
        (spread, own, handled, other, table)
    )
    first = over_chan(pick(spread, handled)).reshape(GROUPS, ROWS, CH)
    second = over_chan(pick(spread, pairing[2])).reshape(GROUPS, ROWS, CH)
    pair_blocks = sent_over_x(correlate(own, first, table, 2))
    last_parts = correlate(own, second, table, 1)
    pair_blocks, last_parts = lax.optimization_barrier((pair_blocks, last_parts))
    pair_halves = sum_of(pair_blocks)
    last_blocks = sent_over_x(last_parts)
    behind = sum_over_y(pair_halves[:, 1])
    behind = over_chan(behind.reshape(N_CHAN, 64, CH).astype(BF16))
    behind = behind.at[other].get(mode="promise_in_bounds")
    last_blocks = lax.optimization_barrier((last_blocks, behind))[0]
    behind = over_chan(behind)
    ahead = sum_over_y(pair_halves[:, 0])
    last = sum_over_y(sum_of(last_blocks)[:, 0])

    def lags_first(value):
        return value.reshape(CH, 8, CH).transpose(1, 0, 2)

    forward = lags_first(ahead)
    backward = behind.astype(F32).reshape(CH, 8, CH).transpose(1, 2, 0)
    mine = lax.dynamic_index_in_dim(handles_zero, lax.axis_index("chan"), 0, keepdims=False)
    return jnp.stack(
        [
            jnp.where(mine, forward, backward),
            jnp.where(mine, backward, forward),
            lags_first(last),
        ]
    )


def solution(mesh):
    return jax.shard_map(
        body,
        mesh=mesh,
        in_specs=(P("chan", "tm", None), P()),
        out_specs=P(None, "tm", "chan", None),
        check_vma=False,
    )
```

profile of v0, /device:TPU:1, one launch (start us, length us, event | category | flops | bytes accessed | tf_op | source)
XLA Modules:
  0.0 243.8 jit_solution(10638337857230997521)
XLA Ops:
  0.0 12.9 %whiten.1.spec = bf16[64,256,128]{2,1,0:T(8,128)(2,1)} custom-call(bf16[128,32,512]{2,1,0:T(8,128)(2,1)} %traces.1, f32[1,512]{1,0:T(1,128)} %constant.78.clone.taper_hbm, bf16[512,512]{1,0:T(8,128)(2,1)} %constant.79.clone.table_hbm), custom_call_target="tpu_custom_call" | custom-call | flops 2147483648 | bytes 8388608 | tf_op jit(solution)/shard_map/whiten/pallas_call | solution.py:119
  12.9 7.9 %all-to-all-start = ((bf16[16,1024,128]{2,1,0:T(8,128)(2,1)}), bf16[16,1024,128]{2,1,0:T(8,128)(2,1)}, u32[]{:S(2)}, u32[]{:S(2)}) async-start(bf16[16,1024,128]{2,1,0:T(8,128)(2,1)} %bitcast.57), calls=%async_computation | async-start | bytes 8388608 | tf_op jit(solution)/shard_map/all_to_all | solution.py:314
  22.0 2.2 copy-done
  24.2 7.1 %expand.1.own_hbm = bf16[64,512,256]{2,1,0:T(8,128)(2,1)S(1)} custom-call(bf16[64,256,128]{2,1,0:T(8,128)(2,1)S(1)} %copy-done), custom_call_target="tpu_custom_call" | custom-call | flops 67108864 | bytes 20971520 | tf_op jit(solution)/shard_map/expand/pallas_call | solution.py:154
  31.3 5.7 %copy-done.1 = bf16[64,512,256]{2,1,0:T(8,128)(2,1)} copy-done((bf16[64,512,256]{2,1,0:T(8,128)(2,1)}, bf16[64,512,256]{2,1,0:T(8,128)(2,1)S(1)}, u32[]{:S(2)}) %copy-start.1) | copy-done | bytes 16777240
  38.5 31.9 %all-to-all-done.source = bf16[16,1024,128]{2,1,0:T(8,128)(2,1)} async-done(((bf16[16,1024,128]{2,1,0:T(8,128)(2,1)}), bf16[16,1024,128]{2,1,0:T(8,128)(2,1)}, u32[]{:S(2)}, u32[]{:S(2)}) %all-to-all-start) | async-done | bytes 4194336 | tf_op jit(solution)/shard_map/all_to_all | solution.py:314
  70.4 4.5 %pick.2 = bf16[16,1024,128]{2,1,0:T(8,128)(2,1)} custom-call(s32[16]{0:T(128)} %fusion.10.index, bf16[16,1024,128]{2,1,0:T(8,128)(2,1)} %all-to-all-done.source), custom_call_target="tpu_custom_call" | custom-call | bytes 8388608 | tf_op jit(solution)/shard_map/pick/pallas_call | solution.py:275
  74.9 5.1 %all-to-all-start.1 = ((bf16[16,1024,128]{2,1,0:T(8,128)(2,1)}), bf16[16,1024,128]{2,1,0:T(8,128)(2,1)}, u32[]{:S(2)}, u32[]{:S(2)}) async-start(bf16[16,1024,128]{2,1,0:T(8,128)(2,1)} %pick.2), calls=%async_computation.1 | async-start | bytes 8388608 | tf_op jit(solution)/shard_map/all_to_all | solution.py:314
  80.1 4.5 %pick.3 = bf16[16,1024,128]{2,1,0:T(8,128)(2,1)} custom-call(s32[16]{0:T(128)} %get-tuple-element.65.index, bf16[16,1024,128]{2,1,0:T(8,128)(2,1)} %all-to-all-done.source), custom_call_target="tpu_custom_call" | custom-call | bytes 8388608 | tf_op jit(solution)/shard_map/pick/pallas_call | solution.py:275
  84.6 45.2 %all-to-all-done.1 = bf16[16,1024,128]{2,1,0:T(8,128)(2,1)} async-done(((bf16[16,1024,128]{2,1,0:T(8,128)(2,1)}), bf16[16,1024,128]{2,1,0:T(8,128)(2,1)}, u32[]{:S(2)}, u32[]{:S(2)}) %all-to-all-start.1) | async-done | bytes 4194336 | tf_op jit(solution)/shard_map/all_to_all | solution.py:314
  129.9 5.2 %all-to-all-start.2 = ((bf16[16,1024,128]{2,1,0:T(8,128)(2,1)}), bf16[16,1024,128]{2,1,0:T(8,128)(2,1)}, u32[]{:S(2)}, u32[]{:S(2)}) async-start(bf16[16,1024,128]{2,1,0:T(8,128)(2,1)} %pick.3), calls=%async_computation.2 | async-start | bytes 8388608 | tf_op jit(solution)/shard_map/all_to_all | solution.py:314
  135.6 13.4 %correlate_both.1 = (bf16[2,2,64,16,128]{4,3,2,1,0:T(8,128)(2,1)}, bf16[2,2,64,16,128]{4,3,2,1,0:T(8,128)(2,1)}, bf16[2,2,64,16,128]{4,3,2,1,0:T(8,128)(2,1)}, bf16[2,2,64,16,128]{4,3,2,1,0:T(8,128)(2,1)}) custom-call(bf16[64,512,256]{2,1,0:T(8,128)(2,1)} %copy-done.1, bf16[64,256,128]{2,1,0:T(8,128)(2,1)} %bitcast.4.partner_hbm, ...), custom_call_target="tpu_custom_call" | custom-call | flops 17179869184 | bytes 25165824 | tf_op jit(solution)/shard_map/correlate_both/pallas_call | solution.py:236
  149.0 2.8 %collective-permute-start = (bf16[2,2,64,16,128]{4,3,2,1,0:T(8,128)(2,1)}, bf16[2,2,64,16,128]{4,3,2,1,0:T(8,128)(2,1)S(1)}, u32[]{:S(2)}, u32[]{:S(2)}) collective-permute-start(bf16[2,2,64,16,128]{4,3,2,1,0:T(8,128)(2,1)} %get-tuple-element.35), channel_id=1, source_target_pairs={{0,4},{1,5},{2,6},{3,7},{4,0},{5,1},{6,2},{7,3},{8,12},{9,13},{10,... | collective-permute-start | bytes 3145736 | tf_op jit(solution)/shard_map/ppermute | solution.py:321
  152.2 2.4 collective-permute-start.2
  154.6 30.3 %all-to-all-done.2 = bf16[16,1024,128]{2,1,0:T(8,128)(2,1)} async-done(((bf16[16,1024,128]{2,1,0:T(8,128)(2,1)}), bf16[16,1024,128]{2,1,0:T(8,128)(2,1)}, u32[]{:S(2)}, u32[]{:S(2)}) %all-to-all-start.2) | async-done | bytes 4194336 | tf_op jit(solution)/shard_map/all_to_all | solution.py:314
  184.8 13.2 %correlate_one.1 = (bf16[2,1,64,16,128]{4,3,2,1,0:T(8,128)(2,1)}, bf16[2,1,64,16,128]{4,3,2,1,0:T(8,128)(2,1)}, bf16[2,1,64,16,128]{4,3,2,1,0:T(8,128)(2,1)}, bf16[2,1,64,16,128]{4,3,2,1,0:T(8,128)(2,1)}) custom-call(bf16[64,512,256]{2,1,0:T(8,128)(2,1)} %copy-done.1, bf16[64,256,128]{2,1,0:T(8,128)(2,1)} %bitcast.6.partner_hbm, ...), custom_call_target="tpu_custom_call" | custom-call | flops 17179869184 | bytes 25165824 | tf_op jit(solution)/shard_map/correlate_one/pallas_call | solution.py:236
  199.1 2.7 %collective-permute-start.4 = (bf16[64,16,128]{2,1,0:T(8,128)(2,1)S(1)}, bf16[64,16,128]{2,1,0:T(8,128)(2,1)S(1)}, u32[]{:S(2)}, u32[]{:S(2)}) collective-permute-start(bf16[64,16,128]{2,1,0:T(8,128)(2,1)S(1)} %fusion.6), channel_id=1, source_target_pairs={{0,1},{1,0},{2,3},{3,2},{4,5},{5,4},{6,7},{7,6},{8,9},{9,8},{10,11... | collective-permute-start | bytes 786440 | tf_op jit(solution)/shard_map/ppermute | solution.py:335
  202.3 2.4 %collective-permute-start.5 = (bf16[2,1,64,16,128]{4,3,2,1,0:T(8,128)(2,1)}, bf16[2,1,64,16,128]{4,3,2,1,0:T(8,128)(2,1)S(1)}, u32[]{:S(2)}, u32[]{:S(2)}) collective-permute-start(bf16[2,1,64,16,128]{4,3,2,1,0:T(8,128)(2,1)} %get-tuple-element.48), channel_id=1, source_target_pairs={{0,4},{1,5},{2,6},{3,7},{4,0},{5,1},{6,2},{7,3},{8,12},{9,13},{10,... | collective-permute-start | bytes 1572872 | tf_op jit(solution)/shard_map/ppermute | solution.py:321
  208.7 8.1 %all-to-all-start.3 = ((bf16[16,64,128]{2,1,0:T(8,128)(2,1)}), bf16[16,64,128]{2,1,0:T(8,128)(2,1)S(1)}, u32[]{:S(2)}, u32[]{:S(2)}) async-start(bf16[16,64,128]{2,1,0:T(8,128)(2,1)} %bitcast.13), calls=%async_computation.3 | async-start | bytes 524288 | tf_op jit(solution)/shard_map/all_to_all | solution.py:314
  217.1 6.8 %all-to-all-done.3 = bf16[16,64,128]{2,1,0:T(8,128)(2,1)S(1)} async-done(((bf16[16,64,128]{2,1,0:T(8,128)(2,1)}), bf16[16,64,128]{2,1,0:T(8,128)(2,1)S(1)}, u32[]{:S(2)}, u32[]{:S(2)}) %all-to-all-start.3) | async-done | bytes 262176 | tf_op jit(solution)/shard_map/all_to_all | solution.py:314
  225.2 4.3 %all-to-all-start.4 = ((bf16[16,64,128]{2,1,0:T(8,128)(2,1)}), bf16[16,64,128]{2,1,0:T(8,128)(2,1)S(1)}, u32[]{:S(2)}, u32[]{:S(2)}) async-start(bf16[16,64,128]{2,1,0:T(8,128)(2,1)} %gather_fusion), calls=%async_computation.4 | async-start | bytes 524288 | tf_op jit(solution)/shard_map/all_to_all | solution.py:314
  231.1 2.7 %collective-permute-start.8 = (bf16[64,16,128]{2,1,0:T(8,128)(2,1)S(1)}, bf16[64,16,128]{2,1,0:T(8,128)(2,1)S(1)}, u32[]{:S(2)}, u32[]{:S(2)}) collective-permute-start(bf16[64,16,128]{2,1,0:T(8,128)(2,1)S(1)} %fusion.7), channel_id=1, source_target_pairs={{0,1},{1,0},{2,3},{3,2},{4,5},{5,4},{6,7},{7,6},{8,9},{9,8},{10,11... | collective-permute-start | bytes 786440 | tf_op jit(solution)/shard_map/ppermute | solution.py:335
  233.8 3.1 %all-to-all-done.4 = bf16[16,64,128]{2,1,0:T(8,128)(2,1)S(1)} async-done(((bf16[16,64,128]{2,1,0:T(8,128)(2,1)}), bf16[16,64,128]{2,1,0:T(8,128)(2,1)S(1)}, u32[]{:S(2)}, u32[]{:S(2)}) %all-to-all-start.4) | async-done | bytes 262176 | tf_op jit(solution)/shard_map/all_to_all | solution.py:314
  237.6 4.1 %collective-permute-done.8 = bf16[64,16,128]{2,1,0:T(8,128)(2,1)S(1)} collective-permute-done((bf16[64,16,128]{2,1,0:T(8,128)(2,1)S(1)}, bf16[64,16,128]{2,1,0:T(8,128)(2,1)S(1)}, u32[]{:S(2)}, u32[]{:S(2)}) %collective-permute-start.8) | collective-permute-done | bytes 262176 | tf_op jit(solution)/shard_map/ppermute | solution.py:335
  (52 shorter events, 14.9 us)
Async XLA Ops:
  12.9 7.9 %copy-start.5 = (s32[3,16]{1,0:T(4,128)S(1)}, s32[3,16]{1,0:T(4,128)}, u32[]{:S(2)}) copy-start(s32[3,16]{1,0:T(4,128)} %param.6) | copy-start | bytes 580
  12.9 57.5 %all-to-all-start = ((bf16[16,1024,128]{2,1,0:T(8,128)(2,1)}), bf16[16,1024,128]{2,1,0:T(8,128)(2,1)}, u32[]{:S(2)}, u32[]{:S(2)}) async-start(bf16[16,1024,128]{2,1,0:T(8,128)(2,1)} %bitcast.57), calls=%async_computation | async-start | bytes 8388608 | tf_op jit(solution)/shard_map/all_to_all | solution.py:314
  22.0 2.2 copy-start
  24.2 13.0 %copy-start.4 = (bf16[2,256,512]{2,1,0:T(8,128)(2,1)S(1)}, bf16[2,256,512]{2,1,0:T(8,128)(2,1)}, u32[]{:S(2)}) copy-start(bf16[2,256,512]{2,1,0:T(8,128)(2,1)} %constant.80.clone) | copy-start | bytes 1572868
  31.3 5.7 %copy-start.1 = (bf16[64,512,256]{2,1,0:T(8,128)(2,1)}, bf16[64,512,256]{2,1,0:T(8,128)(2,1)S(1)}, u32[]{:S(2)}) copy-start(bf16[64,512,256]{2,1,0:T(8,128)(2,1)S(1)} %expand.1.own_hbm) | copy-start | bytes 50331652
  74.9 54.9 %all-to-all-start.1 = ((bf16[16,1024,128]{2,1,0:T(8,128)(2,1)}), bf16[16,1024,128]{2,1,0:T(8,128)(2,1)}, u32[]{:S(2)}, u32[]{:S(2)}) async-start(bf16[16,1024,128]{2,1,0:T(8,128)(2,1)} %pick.2), calls=%async_computation.1 | async-start | bytes 8388608 | tf_op jit(solution)/shard_map/all_to_all | solution.py:314
  129.9 54.9 %all-to-all-start.2 = ((bf16[16,1024,128]{2,1,0:T(8,128)(2,1)}), bf16[16,1024,128]{2,1,0:T(8,128)(2,1)}, u32[]{:S(2)}, u32[]{:S(2)}) async-start(bf16[16,1024,128]{2,1,0:T(8,128)(2,1)} %pick.3), calls=%async_computation.2 | async-start | bytes 8388608 | tf_op jit(solution)/shard_map/all_to_all | solution.py:314
  149.0 49.0 %collective-permute-start = (bf16[2,2,64,16,128]{4,3,2,1,0:T(8,128)(2,1)}, bf16[2,2,64,16,128]{4,3,2,1,0:T(8,128)(2,1)S(1)}, u32[]{:S(2)}, u32[]{:S(2)}) collective-permute-start(bf16[2,2,64,16,128]{4,3,2,1,0:T(8,128)(2,1)} %get-tuple-element.35), channel_id=1, source_target_pairs={{0,4},{1,5},{2,6},{3,7},{4,0},{5,1},{6,2},{7,3},{8,12},{9,13},{10,... | collective-permute-start | bytes 3145736 | tf_op jit(solution)/shard_map/ppermute | solution.py:321
  151.9 46.5 %collective-permute-start.1 = (bf16[2,2,64,16,128]{4,3,2,1,0:T(8,128)(2,1)}, bf16[2,2,64,16,128]{4,3,2,1,0:T(8,128)(2,1)S(1)}, u32[]{:S(2)}, u32[]{:S(2)}) collective-permute-start(bf16[2,2,64,16,128]{4,3,2,1,0:T(8,128)(2,1)} %get-tuple-element.36), channel_id=1, source_target_pairs={{0,2},{1,3},{2,4},{3,5},{4,6},{5,7},{6,0},{7,1},{8,10},{9,11},{10,... | collective-permute-start | bytes 3145736 | tf_op jit(solution)/shard_map/ppermute | solution.py:321
  152.2 46.2 %collective-permute-start.2 = (bf16[2,2,64,16,128]{4,3,2,1,0:T(8,128)(2,1)}, bf16[2,2,64,16,128]{4,3,2,1,0:T(8,128)(2,1)S(1)}, u32[]{:S(2)}, u32[]{:S(2)}) collective-permute-start(bf16[2,2,64,16,128]{4,3,2,1,0:T(8,128)(2,1)} %get-tuple-element.37), channel_id=1, source_target_pairs={{0,6},{1,7},{2,0},{3,1},{4,2},{5,3},{6,4},{7,5},{8,14},{9,15},{10,... | collective-permute-start | bytes 3145736 | tf_op jit(solution)/shard_map/ppermute | solution.py:321
  184.8 13.6 %copy-start.2 = (bf16[2,2,64,16,128]{4,3,2,1,0:T(8,128)(2,1)S(1)}, bf16[2,2,64,16,128]{4,3,2,1,0:T(8,128)(2,1)}, u32[]{:S(2)}) copy-start(bf16[2,2,64,16,128]{4,3,2,1,0:T(8,128)(2,1)} %get-tuple-element.42) | copy-start | bytes 3145732
  199.1 8.8 %collective-permute-start.4 = (bf16[64,16,128]{2,1,0:T(8,128)(2,1)S(1)}, bf16[64,16,128]{2,1,0:T(8,128)(2,1)S(1)}, u32[]{:S(2)}, u32[]{:S(2)}) collective-permute-start(bf16[64,16,128]{2,1,0:T(8,128)(2,1)S(1)} %fusion.6), channel_id=1, source_target_pairs={{0,1},{1,0},{2,3},{3,2},{4,5},{5,4},{6,7},{7,6},{8,9},{9,8},{10,11... | collective-permute-start | bytes 786440 | tf_op jit(solution)/shard_map/ppermute | solution.py:335
  201.8 15.0 %collective-permute-start.3 = (bf16[64,16,128]{2,1,0:T(8,128)(2,1)S(1)}, bf16[64,16,128]{2,1,0:T(8,128)(2,1)S(1)}, u32[]{:S(2)}, u32[]{:S(2)}) collective-permute-start(bf16[64,16,128]{2,1,0:T(8,128)(2,1)S(1)} %fusion.5), channel_id=1, source_target_pairs={{0,1},{1,0},{2,3},{3,2},{4,5},{5,4},{6,7},{7,6},{8,9},{9,8},{10,11... | collective-permute-start | bytes 786440 | tf_op jit(solution)/shard_map/ppermute | solution.py:335
  202.3 27.3 %collective-permute-start.5 = (bf16[2,1,64,16,128]{4,3,2,1,0:T(8,128)(2,1)}, bf16[2,1,64,16,128]{4,3,2,1,0:T(8,128)(2,1)S(1)}, u32[]{:S(2)}, u32[]{:S(2)}) collective-permute-start(bf16[2,1,64,16,128]{4,3,2,1,0:T(8,128)(2,1)} %get-tuple-element.48), channel_id=1, source_target_pairs={{0,4},{1,5},{2,6},{3,7},{4,0},{5,1},{6,2},{7,3},{8,12},{9,13},{10,... | collective-permute-start | bytes 1572872 | tf_op jit(solution)/shard_map/ppermute | solution.py:321
  204.7 24.8 %collective-permute-start.6 = (bf16[2,1,64,16,128]{4,3,2,1,0:T(8,128)(2,1)}, bf16[2,1,64,16,128]{4,3,2,1,0:T(8,128)(2,1)}, u32[]{:S(2)}, u32[]{:S(2)}) collective-permute-start(bf16[2,1,64,16,128]{4,3,2,1,0:T(8,128)(2,1)} %get-tuple-element.49), channel_id=1, source_target_pairs={{0,2},{1,3},{2,4},{3,5},{4,6},{5,7},{6,0},{7,1},{8,10},{9,11},{10,... | collective-permute-start | bytes 1572872 | tf_op jit(solution)/shard_map/ppermute | solution.py:321
  205.3 24.2 %collective-permute-start.7 = (bf16[2,1,64,16,128]{4,3,2,1,0:T(8,128)(2,1)}, bf16[2,1,64,16,128]{4,3,2,1,0:T(8,128)(2,1)}, u32[]{:S(2)}, u32[]{:S(2)}) collective-permute-start(bf16[2,1,64,16,128]{4,3,2,1,0:T(8,128)(2,1)} %get-tuple-element.50), channel_id=1, source_target_pairs={{0,6},{1,7},{2,0},{3,1},{4,2},{5,3},{6,4},{7,5},{8,14},{9,15},{10,... | collective-permute-start | bytes 1572872 | tf_op jit(solution)/shard_map/ppermute | solution.py:321
  208.7 20.9 %copy-start.3 = (bf16[2,1,64,16,128]{4,3,2,1,0:T(8,128)(2,1)S(1)}, bf16[2,1,64,16,128]{4,3,2,1,0:T(8,128)(2,1)}, u32[]{:S(2)}) copy-start(bf16[2,1,64,16,128]{4,3,2,1,0:T(8,128)(2,1)} %get-tuple-element.51) | copy-start | bytes 1572868
  208.7 15.3 %all-to-all-start.3 = ((bf16[16,64,128]{2,1,0:T(8,128)(2,1)}), bf16[16,64,128]{2,1,0:T(8,128)(2,1)S(1)}, u32[]{:S(2)}, u32[]{:S(2)}) async-start(bf16[16,64,128]{2,1,0:T(8,128)(2,1)} %bitcast.13), calls=%async_computation.3 | async-start | bytes 524288 | tf_op jit(solution)/shard_map/all_to_all | solution.py:314
  225.2 11.7 %all-to-all-start.4 = ((bf16[16,64,128]{2,1,0:T(8,128)(2,1)}), bf16[16,64,128]{2,1,0:T(8,128)(2,1)S(1)}, u32[]{:S(2)}, u32[]{:S(2)}) async-start(bf16[16,64,128]{2,1,0:T(8,128)(2,1)} %gather_fusion), calls=%async_computation.4 | async-start | bytes 524288 | tf_op jit(solution)/shard_map/all_to_all | solution.py:314
  231.1 10.7 %collective-permute-start.8 = (bf16[64,16,128]{2,1,0:T(8,128)(2,1)S(1)}, bf16[64,16,128]{2,1,0:T(8,128)(2,1)S(1)}, u32[]{:S(2)}, u32[]{:S(2)}) collective-permute-start(bf16[64,16,128]{2,1,0:T(8,128)(2,1)S(1)} %fusion.7), channel_id=1, source_target_pairs={{0,1},{1,0},{2,3},{3,2},{4,5},{5,4},{6,7},{7,6},{8,9},{9,8},{10,11... | collective-permute-start | bytes 786440 | tf_op jit(solution)/shard_map/ppermute | solution.py:335
where the time goes:
time: 244 us
  waiting for transfers between devices  122 us (50%)
  Pallas kernels  55.7 us (23%)
  starting transfers between devices  47 us (19%)
  local copies, waits for them, and re-layouts  13.5 us (6%)
  other arithmetic  5.04 us (2%)
    all_to_all x5, waiting for transfers between devices, over_chan(): lax.all_to_all(blocks, 'chan', split_axis=0, concat_axis=0, tiled=True)  117 us
    all_to_all x5, starting transfers between devices, over_chan(): lax.all_to_all(blocks, 'chan', split_axis=0, concat_axis=0, tiled=True)  30.6 us
    pallas_call x2, Pallas kernels, correlate(): pl.pallas_call(functools.partial(correlate_kernel, steps), grid=(steps +...  26.7 us
    pallas_call x1, Pallas kernels, whiten(): pl.pallas_call(whiten_kernel, out_shape=jax.ShapeDtypeStruct((GROUPS, ROW...  12.9 us
    ppermute x6, starting transfers between devices, sent_over_x(): got.append(lax.ppermute(parts[shift], 'tm', route))  10.6 us
    pallas_call x2, Pallas kernels, pick(): pl.pallas_call(pick_kernel, grid_spec=pltpu.PrefetchScalarGridSpec(num_sc...  9.05 us
    unnamed x12, local copies, waits for them, and re-layouts  7.93 us
    pallas_call x1, Pallas kernels, expand(): pl.pallas_call(expand_kernel, grid=(GROUPS // per,), out_shape=jax.ShapeD...  7.11 us
  transfers between devices with their start and end apart: 14, of which 8 were waited for; matrix products, arithmetic and copies ran while one was open for 3% of the time, Pallas kernels for 16%

commit v1 on v0

--- a/solution.py
+++ b/solution.py
@@ -49,7 +49,8 @@
     return taper.astype(np.float32).reshape(1, SAMPLES)
 
 
-CHUNK = 16
+CHUNK = 32
+PITCH = 40
 PART = 4
 
 
@@ -81,9 +82,11 @@
             first = chunk * CHUNK + half * 8
             rows = raw[pl.ds(first, 8)].astype(F32)
             rows = rows - jnp.mean(rows, axis=2, keepdims=True)
-            rows = (rows * taper[...].reshape(1, 1, SAMPLES)).reshape(8 * WIN, SAMPLES)
-            for tile in range(4):
-                tapered[tile, pl.ds(first * WIN, 8 * WIN), :] = rows[:, tile * 128 : tile * 128 + 128]
+            rows = rows * taper[...].reshape(1, 1, SAMPLES)
+            for inner in range(8):
+                place = pl.ds((first + inner) * PITCH, WIN)
+                for tile in range(4):
+                    tapered[tile, place, :] = rows[inner, :, tile * 128 : tile * 128 + 128]
         return carry
 
     lax.fori_loop(0, CH // CHUNK, taper_step, 0)
@@ -94,7 +97,8 @@
             columns = []
             for half in range(2):
                 tiles = [
-                    tapered[tile, pl.ds(pair * 2 + half, CH, stride=WIN), :] for tile in range(4)
+                    tapered[tile, pl.ds(pair * 2 + half, CH, stride=PITCH), :]
+                    for tile in range(4)
                 ]
                 columns.append(jnp.concatenate(tiles, axis=1).astype(BF16))
             columns = jnp.concatenate(columns, axis=0)
@@ -125,7 +129,7 @@
             pltpu.VMEM((CH, WIN, SAMPLES), BF16),
             pltpu.VMEM((1, SAMPLES), F32),
             pltpu.VMEM((2 * FREQS, SAMPLES), BF16),
-            pltpu.VMEM((4, CH * WIN, 128), F32),
+            pltpu.VMEM((4, CH * PITCH, 128), F32),
             pltpu.VMEM((GROUPS, ROWS, CH), BF16),
             pltpu.SemaphoreType.DMA((2,)),
             pltpu.SemaphoreType.DMA((CH // CHUNK,)),

time: 244 us -> 240 us (0.984)
  Pallas kernels: 55.7 us -> 51.4 us
    pallas_call x1, Pallas kernels: 12.9 us -> 8.63 us  [whiten(): pl.pallas_call(whiten_kernel, out_shape=jax.ShapeDtypeStruct((GROUPS, ROW...]
where the time goes in v1:
time: 240 us
  waiting for transfers between devices  122 us (51%)
  Pallas kernels  51.4 us (21%)
  starting transfers between devices  47 us (20%)
  local copies, waits for them, and re-layouts  13.5 us (6%)
  other arithmetic  5.04 us (2%)
    all_to_all x5, waiting for transfers between devices, over_chan(): lax.all_to_all(blocks, 'chan', split_axis=0, concat_axis=0, tiled=True)  117 us
    all_to_all x5, starting transfers between devices, over_chan(): lax.all_to_all(blocks, 'chan', split_axis=0, concat_axis=0, tiled=True)  30.6 us
    pallas_call x2, Pallas kernels, correlate(): pl.pallas_call(functools.partial(correlate_kernel, steps), grid=(steps +...  26.7 us
    ppermute x6, starting transfers between devices, sent_over_x(): got.append(lax.ppermute(parts[shift], 'tm', route))  10.6 us
    pallas_call x2, Pallas kernels, pick(): pl.pallas_call(pick_kernel, grid_spec=pltpu.PrefetchScalarGridSpec(num_sc...  9.05 us
    pallas_call x1, Pallas kernels, whiten(): pl.pallas_call(whiten_kernel, out_shape=jax.ShapeDtypeStruct((GROUPS, ROW...  8.63 us
    unnamed x12, local copies, waits for them, and re-layouts  7.93 us
    pallas_call x1, Pallas kernels, expand(): pl.pallas_call(expand_kernel, grid=(GROUPS // per,), out_shape=jax.ShapeD...  7.11 us
  transfers between devices with their start and end apart: 14, of which 8 were waited for; matrix products, arithmetic and copies ran while one was open for 3% of the time, Pallas kernels for 16%

profile of v1, /device:TPU:1, one launch (start us, length us, event | category | flops | bytes accessed | tf_op | source)
XLA Modules:
  0.0 239.6 jit_solution(15649102059945251275)
XLA Ops:
  0.0 8.6 %whiten.1.spec = bf16[64,256,128]{2,1,0:T(8,128)(2,1)} custom-call(bf16[128,32,512]{2,1,0:T(8,128)(2,1)} %traces.1, f32[1,512]{1,0:T(1,128)} %constant.78.clone.taper_hbm, bf16[512,512]{1,0:T(8,128)(2,1)} %constant.79.clone.table_hbm), custom_call_target="tpu_custom_call" | custom-call | flops 2147483648 | bytes 8388608 | tf_op jit(solution)/shard_map/whiten/pallas_call | solution.py:123
  8.6 7.9 %all-to-all-start = ((bf16[16,1024,128]{2,1,0:T(8,128)(2,1)}), bf16[16,1024,128]{2,1,0:T(8,128)(2,1)}, u32[]{:S(2)}, u32[]{:S(2)}) async-start(bf16[16,1024,128]{2,1,0:T(8,128)(2,1)} %bitcast.57), calls=%async_computation | async-start | bytes 8388608 | tf_op jit(solution)/shard_map/all_to_all | solution.py:318
  17.8 2.2 copy-done
  20.0 7.1 %expand.1.own_hbm = bf16[64,512,256]{2,1,0:T(8,128)(2,1)S(1)} custom-call(bf16[64,256,128]{2,1,0:T(8,128)(2,1)S(1)} %copy-done), custom_call_target="tpu_custom_call" | custom-call | flops 67108864 | bytes 20971520 | tf_op jit(solution)/shard_map/expand/pallas_call | solution.py:158
  27.1 5.7 %copy-done.1 = bf16[64,512,256]{2,1,0:T(8,128)(2,1)} copy-done((bf16[64,512,256]{2,1,0:T(8,128)(2,1)}, bf16[64,512,256]{2,1,0:T(8,128)(2,1)S(1)}, u32[]{:S(2)}) %copy-start.1) | copy-done | bytes 16777240
  34.3 31.9 %all-to-all-done.source = bf16[16,1024,128]{2,1,0:T(8,128)(2,1)} async-done(((bf16[16,1024,128]{2,1,0:T(8,128)(2,1)}), bf16[16,1024,128]{2,1,0:T(8,128)(2,1)}, u32[]{:S(2)}, u32[]{:S(2)}) %all-to-all-start) | async-done | bytes 4194336 | tf_op jit(solution)/shard_map/all_to_all | solution.py:318
  66.2 4.5 %pick.2 = bf16[16,1024,128]{2,1,0:T(8,128)(2,1)} custom-call(s32[16]{0:T(128)} %fusion.10.index, bf16[16,1024,128]{2,1,0:T(8,128)(2,1)} %all-to-all-done.source), custom_call_target="tpu_custom_call" | custom-call | bytes 8388608 | tf_op jit(solution)/shard_map/pick/pallas_call | solution.py:279
  70.7 5.1 %all-to-all-start.1 = ((bf16[16,1024,128]{2,1,0:T(8,128)(2,1)}), bf16[16,1024,128]{2,1,0:T(8,128)(2,1)}, u32[]{:S(2)}, u32[]{:S(2)}) async-start(bf16[16,1024,128]{2,1,0:T(8,128)(2,1)} %pick.2), calls=%async_computation.1 | async-start | bytes 8388608 | tf_op jit(solution)/shard_map/all_to_all | solution.py:318
  75.9 4.5 %pick.3 = bf16[16,1024,128]{2,1,0:T(8,128)(2,1)} custom-call(s32[16]{0:T(128)} %get-tuple-element.65.index, bf16[16,1024,128]{2,1,0:T(8,128)(2,1)} %all-to-all-done.source), custom_call_target="tpu_custom_call" | custom-call | bytes 8388608 | tf_op jit(solution)/shard_map/pick/pallas_call | solution.py:279
  80.4 45.2 %all-to-all-done.1 = bf16[16,1024,128]{2,1,0:T(8,128)(2,1)} async-done(((bf16[16,1024,128]{2,1,0:T(8,128)(2,1)}), bf16[16,1024,128]{2,1,0:T(8,128)(2,1)}, u32[]{:S(2)}, u32[]{:S(2)}) %all-to-all-start.1) | async-done | bytes 4194336 | tf_op jit(solution)/shard_map/all_to_all | solution.py:318
  125.6 5.2 %all-to-all-start.2 = ((bf16[16,1024,128]{2,1,0:T(8,128)(2,1)}), bf16[16,1024,128]{2,1,0:T(8,128)(2,1)}, u32[]{:S(2)}, u32[]{:S(2)}) async-start(bf16[16,1024,128]{2,1,0:T(8,128)(2,1)} %pick.3), calls=%async_computation.2 | async-start | bytes 8388608 | tf_op jit(solution)/shard_map/all_to_all | solution.py:318
  131.4 13.4 %correlate_both.1 = (bf16[2,2,64,16,128]{4,3,2,1,0:T(8,128)(2,1)}, bf16[2,2,64,16,128]{4,3,2,1,0:T(8,128)(2,1)}, bf16[2,2,64,16,128]{4,3,2,1,0:T(8,128)(2,1)}, bf16[2,2,64,16,128]{4,3,2,1,0:T(8,128)(2,1)}) custom-call(bf16[64,512,256]{2,1,0:T(8,128)(2,1)} %copy-done.1, bf16[64,256,128]{2,1,0:T(8,128)(2,1)} %bitcast.4.partner_hbm, ...), custom_call_target="tpu_custom_call" | custom-call | flops 17179869184 | bytes 25165824 | tf_op jit(solution)/shard_map/correlate_both/pallas_call | solution.py:240
  144.8 2.8 %collective-permute-start = (bf16[2,2,64,16,128]{4,3,2,1,0:T(8,128)(2,1)}, bf16[2,2,64,16,128]{4,3,2,1,0:T(8,128)(2,1)S(1)}, u32[]{:S(2)}, u32[]{:S(2)}) collective-permute-start(bf16[2,2,64,16,128]{4,3,2,1,0:T(8,128)(2,1)} %get-tuple-element.35), channel_id=1, source_target_pairs={{0,4},{1,5},{2,6},{3,7},{4,0},{5,1},{6,2},{7,3},{8,12},{9,13},{10,... | collective-permute-start | bytes 3145736 | tf_op jit(solution)/shard_map/ppermute | solution.py:325
  148.0 2.4 collective-permute-start.2
  150.3 30.3 %all-to-all-done.2 = bf16[16,1024,128]{2,1,0:T(8,128)(2,1)} async-done(((bf16[16,1024,128]{2,1,0:T(8,128)(2,1)}), bf16[16,1024,128]{2,1,0:T(8,128)(2,1)}, u32[]{:S(2)}, u32[]{:S(2)}) %all-to-all-start.2) | async-done | bytes 4194336 | tf_op jit(solution)/shard_map/all_to_all | solution.py:318
  180.6 13.2 %correlate_one.1 = (bf16[2,1,64,16,128]{4,3,2,1,0:T(8,128)(2,1)}, bf16[2,1,64,16,128]{4,3,2,1,0:T(8,128)(2,1)}, bf16[2,1,64,16,128]{4,3,2,1,0:T(8,128)(2,1)}, bf16[2,1,64,16,128]{4,3,2,1,0:T(8,128)(2,1)}) custom-call(bf16[64,512,256]{2,1,0:T(8,128)(2,1)} %copy-done.1, bf16[64,256,128]{2,1,0:T(8,128)(2,1)} %bitcast.6.partner_hbm, ...), custom_call_target="tpu_custom_call" | custom-call | flops 17179869184 | bytes 25165824 | tf_op jit(solution)/shard_map/correlate_one/pallas_call | solution.py:240
  194.8 2.7 %collective-permute-start.4 = (bf16[64,16,128]{2,1,0:T(8,128)(2,1)S(1)}, bf16[64,16,128]{2,1,0:T(8,128)(2,1)S(1)}, u32[]{:S(2)}, u32[]{:S(2)}) collective-permute-start(bf16[64,16,128]{2,1,0:T(8,128)(2,1)S(1)} %fusion.6), channel_id=1, source_target_pairs={{0,1},{1,0},{2,3},{3,2},{4,5},{5,4},{6,7},{7,6},{8,9},{9,8},{10,11... | collective-permute-start | bytes 786440 | tf_op jit(solution)/shard_map/ppermute | solution.py:339
  198.0 2.4 %collective-permute-start.5 = (bf16[2,1,64,16,128]{4,3,2,1,0:T(8,128)(2,1)}, bf16[2,1,64,16,128]{4,3,2,1,0:T(8,128)(2,1)S(1)}, u32[]{:S(2)}, u32[]{:S(2)}) collective-permute-start(bf16[2,1,64,16,128]{4,3,2,1,0:T(8,128)(2,1)} %get-tuple-element.48), channel_id=1, source_target_pairs={{0,4},{1,5},{2,6},{3,7},{4,0},{5,1},{6,2},{7,3},{8,12},{9,13},{10,... | collective-permute-start | bytes 1572872 | tf_op jit(solution)/shard_map/ppermute | solution.py:325
  204.4 8.1 %all-to-all-start.3 = ((bf16[16,64,128]{2,1,0:T(8,128)(2,1)}), bf16[16,64,128]{2,1,0:T(8,128)(2,1)S(1)}, u32[]{:S(2)}, u32[]{:S(2)}) async-start(bf16[16,64,128]{2,1,0:T(8,128)(2,1)} %bitcast.13), calls=%async_computation.3 | async-start | bytes 524288 | tf_op jit(solution)/shard_map/all_to_all | solution.py:318
  212.9 6.8 %all-to-all-done.3 = bf16[16,64,128]{2,1,0:T(8,128)(2,1)S(1)} async-done(((bf16[16,64,128]{2,1,0:T(8,128)(2,1)}), bf16[16,64,128]{2,1,0:T(8,128)(2,1)S(1)}, u32[]{:S(2)}, u32[]{:S(2)}) %all-to-all-start.3) | async-done | bytes 262176 | tf_op jit(solution)/shard_map/all_to_all | solution.py:318
  221.0 4.3 %all-to-all-start.4 = ((bf16[16,64,128]{2,1,0:T(8,128)(2,1)}), bf16[16,64,128]{2,1,0:T(8,128)(2,1)S(1)}, u32[]{:S(2)}, u32[]{:S(2)}) async-start(bf16[16,64,128]{2,1,0:T(8,128)(2,1)} %gather_fusion), calls=%async_computation.4 | async-start | bytes 524288 | tf_op jit(solution)/shard_map/all_to_all | solution.py:318
  226.8 2.7 %collective-permute-start.8 = (bf16[64,16,128]{2,1,0:T(8,128)(2,1)S(1)}, bf16[64,16,128]{2,1,0:T(8,128)(2,1)S(1)}, u32[]{:S(2)}, u32[]{:S(2)}) collective-permute-start(bf16[64,16,128]{2,1,0:T(8,128)(2,1)S(1)} %fusion.7), channel_id=1, source_target_pairs={{0,1},{1,0},{2,3},{3,2},{4,5},{5,4},{6,7},{7,6},{8,9},{9,8},{10,11... | collective-permute-start | bytes 786440 | tf_op jit(solution)/shard_map/ppermute | solution.py:339
  229.5 3.1 %all-to-all-done.4 = bf16[16,64,128]{2,1,0:T(8,128)(2,1)S(1)} async-done(((bf16[16,64,128]{2,1,0:T(8,128)(2,1)}), bf16[16,64,128]{2,1,0:T(8,128)(2,1)S(1)}, u32[]{:S(2)}, u32[]{:S(2)}) %all-to-all-start.4) | async-done | bytes 262176 | tf_op jit(solution)/shard_map/all_to_all | solution.py:318
  233.3 4.1 %collective-permute-done.8 = bf16[64,16,128]{2,1,0:T(8,128)(2,1)S(1)} collective-permute-done((bf16[64,16,128]{2,1,0:T(8,128)(2,1)S(1)}, bf16[64,16,128]{2,1,0:T(8,128)(2,1)S(1)}, u32[]{:S(2)}, u32[]{:S(2)}) %collective-permute-start.8) | collective-permute-done | bytes 262176 | tf_op jit(solution)/shard_map/ppermute | solution.py:339
  (52 shorter events, 14.9 us)
Async XLA Ops:
  8.6 7.9 %copy-start.5 = (s32[3,16]{1,0:T(4,128)S(1)}, s32[3,16]{1,0:T(4,128)}, u32[]{:S(2)}) copy-start(s32[3,16]{1,0:T(4,128)} %param.6) | copy-start | bytes 580
  8.6 57.5 %all-to-all-start = ((bf16[16,1024,128]{2,1,0:T(8,128)(2,1)}), bf16[16,1024,128]{2,1,0:T(8,128)(2,1)}, u32[]{:S(2)}, u32[]{:S(2)}) async-start(bf16[16,1024,128]{2,1,0:T(8,128)(2,1)} %bitcast.57), calls=%async_computation | async-start | bytes 8388608 | tf_op jit(solution)/shard_map/all_to_all | solution.py:318
  17.8 2.2 copy-start
  20.0 13.0 %copy-start.4 = (bf16[2,256,512]{2,1,0:T(8,128)(2,1)S(1)}, bf16[2,256,512]{2,1,0:T(8,128)(2,1)}, u32[]{:S(2)}) copy-start(bf16[2,256,512]{2,1,0:T(8,128)(2,1)} %constant.80.clone) | copy-start | bytes 1572868
  27.1 5.7 %copy-start.1 = (bf16[64,512,256]{2,1,0:T(8,128)(2,1)}, bf16[64,512,256]{2,1,0:T(8,128)(2,1)S(1)}, u32[]{:S(2)}) copy-start(bf16[64,512,256]{2,1,0:T(8,128)(2,1)S(1)} %expand.1.own_hbm) | copy-start | bytes 50331652
  70.7 54.9 %all-to-all-start.1 = ((bf16[16,1024,128]{2,1,0:T(8,128)(2,1)}), bf16[16,1024,128]{2,1,0:T(8,128)(2,1)}, u32[]{:S(2)}, u32[]{:S(2)}) async-start(bf16[16,1024,128]{2,1,0:T(8,128)(2,1)} %pick.2), calls=%async_computation.1 | async-start | bytes 8388608 | tf_op jit(solution)/shard_map/all_to_all | solution.py:318
  125.6 54.9 %all-to-all-start.2 = ((bf16[16,1024,128]{2,1,0:T(8,128)(2,1)}), bf16[16,1024,128]{2,1,0:T(8,128)(2,1)}, u32[]{:S(2)}, u32[]{:S(2)}) async-start(bf16[16,1024,128]{2,1,0:T(8,128)(2,1)} %pick.3), calls=%async_computation.2 | async-start | bytes 8388608 | tf_op jit(solution)/shard_map/all_to_all | solution.py:318
  144.8 49.0 %collective-permute-start = (bf16[2,2,64,16,128]{4,3,2,1,0:T(8,128)(2,1)}, bf16[2,2,64,16,128]{4,3,2,1,0:T(8,128)(2,1)S(1)}, u32[]{:S(2)}, u32[]{:S(2)}) collective-permute-start(bf16[2,2,64,16,128]{4,3,2,1,0:T(8,128)(2,1)} %get-tuple-element.35), channel_id=1, source_target_pairs={{0,4},{1,5},{2,6},{3,7},{4,0},{5,1},{6,2},{7,3},{8,12},{9,13},{10,... | collective-permute-start | bytes 3145736 | tf_op jit(solution)/shard_map/ppermute | solution.py:325
  147.6 46.5 %collective-permute-start.1 = (bf16[2,2,64,16,128]{4,3,2,1,0:T(8,128)(2,1)}, bf16[2,2,64,16,128]{4,3,2,1,0:T(8,128)(2,1)S(1)}, u32[]{:S(2)}, u32[]{:S(2)}) collective-permute-start(bf16[2,2,64,16,128]{4,3,2,1,0:T(8,128)(2,1)} %get-tuple-element.36), channel_id=1, source_target_pairs={{0,2},{1,3},{2,4},{3,5},{4,6},{5,7},{6,0},{7,1},{8,10},{9,11},{10,... | collective-permute-start | bytes 3145736 | tf_op jit(solution)/shard_map/ppermute | solution.py:325
  148.0 46.2 %collective-permute-start.2 = (bf16[2,2,64,16,128]{4,3,2,1,0:T(8,128)(2,1)}, bf16[2,2,64,16,128]{4,3,2,1,0:T(8,128)(2,1)S(1)}, u32[]{:S(2)}, u32[]{:S(2)}) collective-permute-start(bf16[2,2,64,16,128]{4,3,2,1,0:T(8,128)(2,1)} %get-tuple-element.37), channel_id=1, source_target_pairs={{0,6},{1,7},{2,0},{3,1},{4,2},{5,3},{6,4},{7,5},{8,14},{9,15},{10,... | collective-permute-start | bytes 3145736 | tf_op jit(solution)/shard_map/ppermute | solution.py:325
  180.6 13.6 %copy-start.2 = (bf16[2,2,64,16,128]{4,3,2,1,0:T(8,128)(2,1)S(1)}, bf16[2,2,64,16,128]{4,3,2,1,0:T(8,128)(2,1)}, u32[]{:S(2)}) copy-start(bf16[2,2,64,16,128]{4,3,2,1,0:T(8,128)(2,1)} %get-tuple-element.42) | copy-start | bytes 3145732
  194.8 8.8 %collective-permute-start.4 = (bf16[64,16,128]{2,1,0:T(8,128)(2,1)S(1)}, bf16[64,16,128]{2,1,0:T(8,128)(2,1)S(1)}, u32[]{:S(2)}, u32[]{:S(2)}) collective-permute-start(bf16[64,16,128]{2,1,0:T(8,128)(2,1)S(1)} %fusion.6), channel_id=1, source_target_pairs={{0,1},{1,0},{2,3},{3,2},{4,5},{5,4},{6,7},{7,6},{8,9},{9,8},{10,11... | collective-permute-start | bytes 786440 | tf_op jit(solution)/shard_map/ppermute | solution.py:339
  197.6 15.0 %collective-permute-start.3 = (bf16[64,16,128]{2,1,0:T(8,128)(2,1)S(1)}, bf16[64,16,128]{2,1,0:T(8,128)(2,1)S(1)}, u32[]{:S(2)}, u32[]{:S(2)}) collective-permute-start(bf16[64,16,128]{2,1,0:T(8,128)(2,1)S(1)} %fusion.5), channel_id=1, source_target_pairs={{0,1},{1,0},{2,3},{3,2},{4,5},{5,4},{6,7},{7,6},{8,9},{9,8},{10,11... | collective-permute-start | bytes 786440 | tf_op jit(solution)/shard_map/ppermute | solution.py:339
  198.0 27.3 %collective-permute-start.5 = (bf16[2,1,64,16,128]{4,3,2,1,0:T(8,128)(2,1)}, bf16[2,1,64,16,128]{4,3,2,1,0:T(8,128)(2,1)S(1)}, u32[]{:S(2)}, u32[]{:S(2)}) collective-permute-start(bf16[2,1,64,16,128]{4,3,2,1,0:T(8,128)(2,1)} %get-tuple-element.48), channel_id=1, source_target_pairs={{0,4},{1,5},{2,6},{3,7},{4,0},{5,1},{6,2},{7,3},{8,12},{9,13},{10,... | collective-permute-start | bytes 1572872 | tf_op jit(solution)/shard_map/ppermute | solution.py:325
  200.5 24.8 %collective-permute-start.6 = (bf16[2,1,64,16,128]{4,3,2,1,0:T(8,128)(2,1)}, bf16[2,1,64,16,128]{4,3,2,1,0:T(8,128)(2,1)}, u32[]{:S(2)}, u32[]{:S(2)}) collective-permute-start(bf16[2,1,64,16,128]{4,3,2,1,0:T(8,128)(2,1)} %get-tuple-element.49), channel_id=1, source_target_pairs={{0,2},{1,3},{2,4},{3,5},{4,6},{5,7},{6,0},{7,1},{8,10},{9,11},{10,... | collective-permute-start | bytes 1572872 | tf_op jit(solution)/shard_map/ppermute | solution.py:325
  201.1 24.2 %collective-permute-start.7 = (bf16[2,1,64,16,128]{4,3,2,1,0:T(8,128)(2,1)}, bf16[2,1,64,16,128]{4,3,2,1,0:T(8,128)(2,1)}, u32[]{:S(2)}, u32[]{:S(2)}) collective-permute-start(bf16[2,1,64,16,128]{4,3,2,1,0:T(8,128)(2,1)} %get-tuple-element.50), channel_id=1, source_target_pairs={{0,6},{1,7},{2,0},{3,1},{4,2},{5,3},{6,4},{7,5},{8,14},{9,15},{10,... | collective-permute-start | bytes 1572872 | tf_op jit(solution)/shard_map/ppermute | solution.py:325
  204.4 20.9 %copy-start.3 = (bf16[2,1,64,16,128]{4,3,2,1,0:T(8,128)(2,1)S(1)}, bf16[2,1,64,16,128]{4,3,2,1,0:T(8,128)(2,1)}, u32[]{:S(2)}) copy-start(bf16[2,1,64,16,128]{4,3,2,1,0:T(8,128)(2,1)} %get-tuple-element.51) | copy-start | bytes 1572868
  204.4 15.3 %all-to-all-start.3 = ((bf16[16,64,128]{2,1,0:T(8,128)(2,1)}), bf16[16,64,128]{2,1,0:T(8,128)(2,1)S(1)}, u32[]{:S(2)}, u32[]{:S(2)}) async-start(bf16[16,64,128]{2,1,0:T(8,128)(2,1)} %bitcast.13), calls=%async_computation.3 | async-start | bytes 524288 | tf_op jit(solution)/shard_map/all_to_all | solution.py:318
  221.0 11.7 %all-to-all-start.4 = ((bf16[16,64,128]{2,1,0:T(8,128)(2,1)}), bf16[16,64,128]{2,1,0:T(8,128)(2,1)S(1)}, u32[]{:S(2)}, u32[]{:S(2)}) async-start(bf16[16,64,128]{2,1,0:T(8,128)(2,1)} %gather_fusion), calls=%async_computation.4 | async-start | bytes 524288 | tf_op jit(solution)/shard_map/all_to_all | solution.py:318
  226.8 10.6 %collective-permute-start.8 = (bf16[64,16,128]{2,1,0:T(8,128)(2,1)S(1)}, bf16[64,16,128]{2,1,0:T(8,128)(2,1)S(1)}, u32[]{:S(2)}, u32[]{:S(2)}) collective-permute-start(bf16[64,16,128]{2,1,0:T(8,128)(2,1)S(1)} %fusion.7), channel_id=1, source_target_pairs={{0,1},{1,0},{2,3},{3,2},{4,5},{5,4},{6,7},{7,6},{8,9},{9,8},{10,11... | collective-permute-start | bytes 786440 | tf_op jit(solution)/shard_map/ppermute | solution.py:339

commit v2 on v1

--- a/solution.py
+++ b/solution.py
@@ -360,7 +360,6 @@
     behind = sum_over_y(pair_halves[:, 1])
     behind = over_chan(behind.reshape(N_CHAN, 64, CH).astype(BF16))
     behind = behind.at[other].get(mode="promise_in_bounds")
-    last_blocks = lax.optimization_barrier((last_blocks, behind))[0]
     behind = over_chan(behind)
     ahead = sum_over_y(pair_halves[:, 0])
     last = sum_over_y(sum_of(last_blocks)[:, 0])

time: 240 us -> 240 us (level)
  no operation moved by 1% of the time
where the time goes in v2:
time: 240 us
  waiting for transfers between devices  122 us (51%)
  Pallas kernels  51.4 us (21%)
  starting transfers between devices  47 us (20%)
  local copies, waits for them, and re-layouts  13.5 us (6%)
  other arithmetic  5.04 us (2%)
    all_to_all x5, waiting for transfers between devices, over_chan(): lax.all_to_all(blocks, 'chan', split_axis=0, concat_axis=0, tiled=True)  117 us
    all_to_all x5, starting transfers between devices, over_chan(): lax.all_to_all(blocks, 'chan', split_axis=0, concat_axis=0, tiled=True)  30.6 us
    pallas_call x2, Pallas kernels, correlate(): pl.pallas_call(functools.partial(correlate_kernel, steps), grid=(steps +...  26.7 us
    ppermute x6, starting transfers between devices, sent_over_x(): got.append(lax.ppermute(parts[shift], 'tm', route))  10.6 us
    pallas_call x2, Pallas kernels, pick(): pl.pallas_call(pick_kernel, grid_spec=pltpu.PrefetchScalarGridSpec(num_sc...  9.05 us
    pallas_call x1, Pallas kernels, whiten(): pl.pallas_call(whiten_kernel, out_shape=jax.ShapeDtypeStruct((GROUPS, ROW...  8.63 us
    unnamed x12, local copies, waits for them, and re-layouts  7.93 us
    pallas_call x1, Pallas kernels, expand(): pl.pallas_call(expand_kernel, grid=(GROUPS // per,), out_shape=jax.ShapeD...  7.11 us
  transfers between devices with their start and end apart: 14, of which 8 were waited for; matrix products, arithmetic and copies ran while one was open for 3% of the time, Pallas kernels for 16%

profile of v2, /device:TPU:1, one launch (start us, length us, event | category | flops | bytes accessed | tf_op | source)
XLA Modules:
  0.0 239.6 jit_solution(15649102059945251275)
XLA Ops:
  0.0 8.6 %whiten.1.spec = bf16[64,256,128]{2,1,0:T(8,128)(2,1)} custom-call(bf16[128,32,512]{2,1,0:T(8,128)(2,1)} %traces.1, f32[1,512]{1,0:T(1,128)} %constant.78.clone.taper_hbm, bf16[512,512]{1,0:T(8,128)(2,1)} %constant.79.clone.table_hbm), custom_call_target="tpu_custom_call" | custom-call | flops 2147483648 | bytes 8388608 | tf_op jit(solution)/shard_map/whiten/pallas_call | solution.py:123
  8.6 7.9 %all-to-all-start = ((bf16[16,1024,128]{2,1,0:T(8,128)(2,1)}), bf16[16,1024,128]{2,1,0:T(8,128)(2,1)}, u32[]{:S(2)}, u32[]{:S(2)}) async-start(bf16[16,1024,128]{2,1,0:T(8,128)(2,1)} %bitcast.57), calls=%async_computation | async-start | bytes 8388608 | tf_op jit(solution)/shard_map/all_to_all | solution.py:318
  17.8 2.2 copy-done
  20.0 7.1 %expand.1.own_hbm = bf16[64,512,256]{2,1,0:T(8,128)(2,1)S(1)} custom-call(bf16[64,256,128]{2,1,0:T(8,128)(2,1)S(1)} %copy-done), custom_call_target="tpu_custom_call" | custom-call | flops 67108864 | bytes 20971520 | tf_op jit(solution)/shard_map/expand/pallas_call | solution.py:158
  27.1 5.7 %copy-done.1 = bf16[64,512,256]{2,1,0:T(8,128)(2,1)} copy-done((bf16[64,512,256]{2,1,0:T(8,128)(2,1)}, bf16[64,512,256]{2,1,0:T(8,128)(2,1)S(1)}, u32[]{:S(2)}) %copy-start.1) | copy-done | bytes 16777240
  34.3 31.9 %all-to-all-done.source = bf16[16,1024,128]{2,1,0:T(8,128)(2,1)} async-done(((bf16[16,1024,128]{2,1,0:T(8,128)(2,1)}), bf16[16,1024,128]{2,1,0:T(8,128)(2,1)}, u32[]{:S(2)}, u32[]{:S(2)}) %all-to-all-start) | async-done | bytes 4194336 | tf_op jit(solution)/shard_map/all_to_all | solution.py:318
  66.2 4.5 %pick.2 = bf16[16,1024,128]{2,1,0:T(8,128)(2,1)} custom-call(s32[16]{0:T(128)} %fusion.10.index, bf16[16,1024,128]{2,1,0:T(8,128)(2,1)} %all-to-all-done.source), custom_call_target="tpu_custom_call" | custom-call | bytes 8388608 | tf_op jit(solution)/shard_map/pick/pallas_call | solution.py:279
  70.7 5.1 %all-to-all-start.1 = ((bf16[16,1024,128]{2,1,0:T(8,128)(2,1)}), bf16[16,1024,128]{2,1,0:T(8,128)(2,1)}, u32[]{:S(2)}, u32[]{:S(2)}) async-start(bf16[16,1024,128]{2,1,0:T(8,128)(2,1)} %pick.2), calls=%async_computation.1 | async-start | bytes 8388608 | tf_op jit(solution)/shard_map/all_to_all | solution.py:318
  75.9 4.5 %pick.3 = bf16[16,1024,128]{2,1,0:T(8,128)(2,1)} custom-call(s32[16]{0:T(128)} %get-tuple-element.57.index, bf16[16,1024,128]{2,1,0:T(8,128)(2,1)} %all-to-all-done.source), custom_call_target="tpu_custom_call" | custom-call | bytes 8388608 | tf_op jit(solution)/shard_map/pick/pallas_call | solution.py:279
  80.4 45.2 %all-to-all-done.1 = bf16[16,1024,128]{2,1,0:T(8,128)(2,1)} async-done(((bf16[16,1024,128]{2,1,0:T(8,128)(2,1)}), bf16[16,1024,128]{2,1,0:T(8,128)(2,1)}, u32[]{:S(2)}, u32[]{:S(2)}) %all-to-all-start.1) | async-done | bytes 4194336 | tf_op jit(solution)/shard_map/all_to_all | solution.py:318
  125.6 5.2 %all-to-all-start.2 = ((bf16[16,1024,128]{2,1,0:T(8,128)(2,1)}), bf16[16,1024,128]{2,1,0:T(8,128)(2,1)}, u32[]{:S(2)}, u32[]{:S(2)}) async-start(bf16[16,1024,128]{2,1,0:T(8,128)(2,1)} %pick.3), calls=%async_computation.2 | async-start | bytes 8388608 | tf_op jit(solution)/shard_map/all_to_all | solution.py:318
  131.4 13.4 %correlate_both.1 = (bf16[2,2,64,16,128]{4,3,2,1,0:T(8,128)(2,1)}, bf16[2,2,64,16,128]{4,3,2,1,0:T(8,128)(2,1)}, bf16[2,2,64,16,128]{4,3,2,1,0:T(8,128)(2,1)}, bf16[2,2,64,16,128]{4,3,2,1,0:T(8,128)(2,1)}) custom-call(bf16[64,512,256]{2,1,0:T(8,128)(2,1)} %copy-done.1, bf16[64,256,128]{2,1,0:T(8,128)(2,1)} %bitcast.4.partner_hbm, ...), custom_call_target="tpu_custom_call" | custom-call | flops 17179869184 | bytes 25165824 | tf_op jit(solution)/shard_map/correlate_both/pallas_call | solution.py:240
  144.8 2.8 %collective-permute-start = (bf16[2,2,64,16,128]{4,3,2,1,0:T(8,128)(2,1)}, bf16[2,2,64,16,128]{4,3,2,1,0:T(8,128)(2,1)S(1)}, u32[]{:S(2)}, u32[]{:S(2)}) collective-permute-start(bf16[2,2,64,16,128]{4,3,2,1,0:T(8,128)(2,1)} %get-tuple-element.31), channel_id=1, source_target_pairs={{0,4},{1,5},{2,6},{3,7},{4,0},{5,1},{6,2},{7,3},{8,12},{9,13},{10,... | collective-permute-start | bytes 3145736 | tf_op jit(solution)/shard_map/ppermute | solution.py:325
  148.0 2.4 collective-permute-start.2
  150.3 30.3 %all-to-all-done.2 = bf16[16,1024,128]{2,1,0:T(8,128)(2,1)} async-done(((bf16[16,1024,128]{2,1,0:T(8,128)(2,1)}), bf16[16,1024,128]{2,1,0:T(8,128)(2,1)}, u32[]{:S(2)}, u32[]{:S(2)}) %all-to-all-start.2) | async-done | bytes 4194336 | tf_op jit(solution)/shard_map/all_to_all | solution.py:318
  180.6 13.2 %correlate_one.1 = (bf16[2,1,64,16,128]{4,3,2,1,0:T(8,128)(2,1)}, bf16[2,1,64,16,128]{4,3,2,1,0:T(8,128)(2,1)}, bf16[2,1,64,16,128]{4,3,2,1,0:T(8,128)(2,1)}, bf16[2,1,64,16,128]{4,3,2,1,0:T(8,128)(2,1)}) custom-call(bf16[64,512,256]{2,1,0:T(8,128)(2,1)} %copy-done.1, bf16[64,256,128]{2,1,0:T(8,128)(2,1)} %bitcast.6.partner_hbm, ...), custom_call_target="tpu_custom_call" | custom-call | flops 17179869184 | bytes 25165824 | tf_op jit(solution)/shard_map/correlate_one/pallas_call | solution.py:240
  194.8 2.7 %collective-permute-start.4 = (bf16[64,16,128]{2,1,0:T(8,128)(2,1)S(1)}, bf16[64,16,128]{2,1,0:T(8,128)(2,1)S(1)}, u32[]{:S(2)}, u32[]{:S(2)}) collective-permute-start(bf16[64,16,128]{2,1,0:T(8,128)(2,1)S(1)} %fusion.6), channel_id=1, source_target_pairs={{0,1},{1,0},{2,3},{3,2},{4,5},{5,4},{6,7},{7,6},{8,9},{9,8},{10,11... | collective-permute-start | bytes 786440 | tf_op jit(solution)/shard_map/ppermute | solution.py:339
  198.0 2.4 %collective-permute-start.5 = (bf16[2,1,64,16,128]{4,3,2,1,0:T(8,128)(2,1)}, bf16[2,1,64,16,128]{4,3,2,1,0:T(8,128)(2,1)S(1)}, u32[]{:S(2)}, u32[]{:S(2)}) collective-permute-start(bf16[2,1,64,16,128]{4,3,2,1,0:T(8,128)(2,1)} %get-tuple-element.44), channel_id=1, source_target_pairs={{0,4},{1,5},{2,6},{3,7},{4,0},{5,1},{6,2},{7,3},{8,12},{9,13},{10,... | collective-permute-start | bytes 1572872 | tf_op jit(solution)/shard_map/ppermute | solution.py:325
  204.4 8.1 %all-to-all-start.3 = ((bf16[16,64,128]{2,1,0:T(8,128)(2,1)}), bf16[16,64,128]{2,1,0:T(8,128)(2,1)S(1)}, u32[]{:S(2)}, u32[]{:S(2)}) async-start(bf16[16,64,128]{2,1,0:T(8,128)(2,1)} %bitcast.13), calls=%async_computation.3 | async-start | bytes 524288 | tf_op jit(solution)/shard_map/all_to_all | solution.py:318
  212.9 6.8 %all-to-all-done.3 = bf16[16,64,128]{2,1,0:T(8,128)(2,1)S(1)} async-done(((bf16[16,64,128]{2,1,0:T(8,128)(2,1)}), bf16[16,64,128]{2,1,0:T(8,128)(2,1)S(1)}, u32[]{:S(2)}, u32[]{:S(2)}) %all-to-all-start.3) | async-done | bytes 262176 | tf_op jit(solution)/shard_map/all_to_all | solution.py:318
  221.0 4.3 %all-to-all-start.4 = ((bf16[16,64,128]{2,1,0:T(8,128)(2,1)}), bf16[16,64,128]{2,1,0:T(8,128)(2,1)S(1)}, u32[]{:S(2)}, u32[]{:S(2)}) async-start(bf16[16,64,128]{2,1,0:T(8,128)(2,1)} %gather_fusion), calls=%async_computation.4 | async-start | bytes 524288 | tf_op jit(solution)/shard_map/all_to_all | solution.py:318
  226.8 2.7 %collective-permute-start.8 = (bf16[64,16,128]{2,1,0:T(8,128)(2,1)S(1)}, bf16[64,16,128]{2,1,0:T(8,128)(2,1)S(1)}, u32[]{:S(2)}, u32[]{:S(2)}) collective-permute-start(bf16[64,16,128]{2,1,0:T(8,128)(2,1)S(1)} %fusion.7), channel_id=1, source_target_pairs={{0,1},{1,0},{2,3},{3,2},{4,5},{5,4},{6,7},{7,6},{8,9},{9,8},{10,11... | collective-permute-start | bytes 786440 | tf_op jit(solution)/shard_map/ppermute | solution.py:339
  229.5 3.1 %all-to-all-done.4 = bf16[16,64,128]{2,1,0:T(8,128)(2,1)S(1)} async-done(((bf16[16,64,128]{2,1,0:T(8,128)(2,1)}), bf16[16,64,128]{2,1,0:T(8,128)(2,1)S(1)}, u32[]{:S(2)}, u32[]{:S(2)}) %all-to-all-start.4) | async-done | bytes 262176 | tf_op jit(solution)/shard_map/all_to_all | solution.py:318
  233.3 4.1 %collective-permute-done.8 = bf16[64,16,128]{2,1,0:T(8,128)(2,1)S(1)} collective-permute-done((bf16[64,16,128]{2,1,0:T(8,128)(2,1)S(1)}, bf16[64,16,128]{2,1,0:T(8,128)(2,1)S(1)}, u32[]{:S(2)}, u32[]{:S(2)}) %collective-permute-start.8) | collective-permute-done | bytes 262176 | tf_op jit(solution)/shard_map/ppermute | solution.py:339
  (52 shorter events, 14.9 us)
Async XLA Ops:
  8.6 7.9 %copy-start.5 = (s32[3,16]{1,0:T(4,128)S(1)}, s32[3,16]{1,0:T(4,128)}, u32[]{:S(2)}) copy-start(s32[3,16]{1,0:T(4,128)} %param.6) | copy-start | bytes 580
  8.6 57.5 %all-to-all-start = ((bf16[16,1024,128]{2,1,0:T(8,128)(2,1)}), bf16[16,1024,128]{2,1,0:T(8,128)(2,1)}, u32[]{:S(2)}, u32[]{:S(2)}) async-start(bf16[16,1024,128]{2,1,0:T(8,128)(2,1)} %bitcast.57), calls=%async_computation | async-start | bytes 8388608 | tf_op jit(solution)/shard_map/all_to_all | solution.py:318
  17.8 2.2 copy-start
  20.0 13.0 %copy-start.4 = (bf16[2,256,512]{2,1,0:T(8,128)(2,1)S(1)}, bf16[2,256,512]{2,1,0:T(8,128)(2,1)}, u32[]{:S(2)}) copy-start(bf16[2,256,512]{2,1,0:T(8,128)(2,1)} %constant.80.clone) | copy-start | bytes 1572868
  27.1 5.7 %copy-start.1 = (bf16[64,512,256]{2,1,0:T(8,128)(2,1)}, bf16[64,512,256]{2,1,0:T(8,128)(2,1)S(1)}, u32[]{:S(2)}) copy-start(bf16[64,512,256]{2,1,0:T(8,128)(2,1)S(1)} %expand.1.own_hbm) | copy-start | bytes 50331652
  70.7 54.9 %all-to-all-start.1 = ((bf16[16,1024,128]{2,1,0:T(8,128)(2,1)}), bf16[16,1024,128]{2,1,0:T(8,128)(2,1)}, u32[]{:S(2)}, u32[]{:S(2)}) async-start(bf16[16,1024,128]{2,1,0:T(8,128)(2,1)} %pick.2), calls=%async_computation.1 | async-start | bytes 8388608 | tf_op jit(solution)/shard_map/all_to_all | solution.py:318
  125.6 54.9 %all-to-all-start.2 = ((bf16[16,1024,128]{2,1,0:T(8,128)(2,1)}), bf16[16,1024,128]{2,1,0:T(8,128)(2,1)}, u32[]{:S(2)}, u32[]{:S(2)}) async-start(bf16[16,1024,128]{2,1,0:T(8,128)(2,1)} %pick.3), calls=%async_computation.2 | async-start | bytes 8388608 | tf_op jit(solution)/shard_map/all_to_all | solution.py:318
  144.8 49.0 %collective-permute-start = (bf16[2,2,64,16,128]{4,3,2,1,0:T(8,128)(2,1)}, bf16[2,2,64,16,128]{4,3,2,1,0:T(8,128)(2,1)S(1)}, u32[]{:S(2)}, u32[]{:S(2)}) collective-permute-start(bf16[2,2,64,16,128]{4,3,2,1,0:T(8,128)(2,1)} %get-tuple-element.31), channel_id=1, source_target_pairs={{0,4},{1,5},{2,6},{3,7},{4,0},{5,1},{6,2},{7,3},{8,12},{9,13},{10,... | collective-permute-start | bytes 3145736 | tf_op jit(solution)/shard_map/ppermute | solution.py:325
  147.6 46.5 %collective-permute-start.1 = (bf16[2,2,64,16,128]{4,3,2,1,0:T(8,128)(2,1)}, bf16[2,2,64,16,128]{4,3,2,1,0:T(8,128)(2,1)S(1)}, u32[]{:S(2)}, u32[]{:S(2)}) collective-permute-start(bf16[2,2,64,16,128]{4,3,2,1,0:T(8,128)(2,1)} %get-tuple-element.32), channel_id=1, source_target_pairs={{0,2},{1,3},{2,4},{3,5},{4,6},{5,7},{6,0},{7,1},{8,10},{9,11},{10,... | collective-permute-start | bytes 3145736 | tf_op jit(solution)/shard_map/ppermute | solution.py:325
  148.0 46.2 %collective-permute-start.2 = (bf16[2,2,64,16,128]{4,3,2,1,0:T(8,128)(2,1)}, bf16[2,2,64,16,128]{4,3,2,1,0:T(8,128)(2,1)S(1)}, u32[]{:S(2)}, u32[]{:S(2)}) collective-permute-start(bf16[2,2,64,16,128]{4,3,2,1,0:T(8,128)(2,1)} %get-tuple-element.33), channel_id=1, source_target_pairs={{0,6},{1,7},{2,0},{3,1},{4,2},{5,3},{6,4},{7,5},{8,14},{9,15},{10,... | collective-permute-start | bytes 3145736 | tf_op jit(solution)/shard_map/ppermute | solution.py:325
  180.6 13.6 %copy-start.2 = (bf16[2,2,64,16,128]{4,3,2,1,0:T(8,128)(2,1)S(1)}, bf16[2,2,64,16,128]{4,3,2,1,0:T(8,128)(2,1)}, u32[]{:S(2)}) copy-start(bf16[2,2,64,16,128]{4,3,2,1,0:T(8,128)(2,1)} %get-tuple-element.38) | copy-start | bytes 3145732
  194.8 8.8 %collective-permute-start.4 = (bf16[64,16,128]{2,1,0:T(8,128)(2,1)S(1)}, bf16[64,16,128]{2,1,0:T(8,128)(2,1)S(1)}, u32[]{:S(2)}, u32[]{:S(2)}) collective-permute-start(bf16[64,16,128]{2,1,0:T(8,128)(2,1)S(1)} %fusion.6), channel_id=1, source_target_pairs={{0,1},{1,0},{2,3},{3,2},{4,5},{5,4},{6,7},{7,6},{8,9},{9,8},{10,11... | collective-permute-start | bytes 786440 | tf_op jit(solution)/shard_map/ppermute | solution.py:339
  197.6 15.0 %collective-permute-start.3 = (bf16[64,16,128]{2,1,0:T(8,128)(2,1)S(1)}, bf16[64,16,128]{2,1,0:T(8,128)(2,1)S(1)}, u32[]{:S(2)}, u32[]{:S(2)}) collective-permute-start(bf16[64,16,128]{2,1,0:T(8,128)(2,1)S(1)} %fusion.5), channel_id=1, source_target_pairs={{0,1},{1,0},{2,3},{3,2},{4,5},{5,4},{6,7},{7,6},{8,9},{9,8},{10,11... | collective-permute-start | bytes 786440 | tf_op jit(solution)/shard_map/ppermute | solution.py:339
  198.0 27.3 %collective-permute-start.5 = (bf16[2,1,64,16,128]{4,3,2,1,0:T(8,128)(2,1)}, bf16[2,1,64,16,128]{4,3,2,1,0:T(8,128)(2,1)S(1)}, u32[]{:S(2)}, u32[]{:S(2)}) collective-permute-start(bf16[2,1,64,16,128]{4,3,2,1,0:T(8,128)(2,1)} %get-tuple-element.44), channel_id=1, source_target_pairs={{0,4},{1,5},{2,6},{3,7},{4,0},{5,1},{6,2},{7,3},{8,12},{9,13},{10,... | collective-permute-start | bytes 1572872 | tf_op jit(solution)/shard_map/ppermute | solution.py:325
  200.5 24.8 %collective-permute-start.6 = (bf16[2,1,64,16,128]{4,3,2,1,0:T(8,128)(2,1)}, bf16[2,1,64,16,128]{4,3,2,1,0:T(8,128)(2,1)}, u32[]{:S(2)}, u32[]{:S(2)}) collective-permute-start(bf16[2,1,64,16,128]{4,3,2,1,0:T(8,128)(2,1)} %get-tuple-element.45), channel_id=1, source_target_pairs={{0,2},{1,3},{2,4},{3,5},{4,6},{5,7},{6,0},{7,1},{8,10},{9,11},{10,... | collective-permute-start | bytes 1572872 | tf_op jit(solution)/shard_map/ppermute | solution.py:325
  201.1 24.2 %collective-permute-start.7 = (bf16[2,1,64,16,128]{4,3,2,1,0:T(8,128)(2,1)}, bf16[2,1,64,16,128]{4,3,2,1,0:T(8,128)(2,1)}, u32[]{:S(2)}, u32[]{:S(2)}) collective-permute-start(bf16[2,1,64,16,128]{4,3,2,1,0:T(8,128)(2,1)} %get-tuple-element.46), channel_id=1, source_target_pairs={{0,6},{1,7},{2,0},{3,1},{4,2},{5,3},{6,4},{7,5},{8,14},{9,15},{10,... | collective-permute-start | bytes 1572872 | tf_op jit(solution)/shard_map/ppermute | solution.py:325
  204.4 20.9 %copy-start.3 = (bf16[2,1,64,16,128]{4,3,2,1,0:T(8,128)(2,1)S(1)}, bf16[2,1,64,16,128]{4,3,2,1,0:T(8,128)(2,1)}, u32[]{:S(2)}) copy-start(bf16[2,1,64,16,128]{4,3,2,1,0:T(8,128)(2,1)} %get-tuple-element.43) | copy-start | bytes 1572868
  204.4 15.3 %all-to-all-start.3 = ((bf16[16,64,128]{2,1,0:T(8,128)(2,1)}), bf16[16,64,128]{2,1,0:T(8,128)(2,1)S(1)}, u32[]{:S(2)}, u32[]{:S(2)}) async-start(bf16[16,64,128]{2,1,0:T(8,128)(2,1)} %bitcast.13), calls=%async_computation.3 | async-start | bytes 524288 | tf_op jit(solution)/shard_map/all_to_all | solution.py:318
  221.0 11.7 %all-to-all-start.4 = ((bf16[16,64,128]{2,1,0:T(8,128)(2,1)}), bf16[16,64,128]{2,1,0:T(8,128)(2,1)S(1)}, u32[]{:S(2)}, u32[]{:S(2)}) async-start(bf16[16,64,128]{2,1,0:T(8,128)(2,1)} %gather_fusion), calls=%async_computation.4 | async-start | bytes 524288 | tf_op jit(solution)/shard_map/all_to_all | solution.py:318
  226.8 10.6 %collective-permute-start.8 = (bf16[64,16,128]{2,1,0:T(8,128)(2,1)S(1)}, bf16[64,16,128]{2,1,0:T(8,128)(2,1)S(1)}, u32[]{:S(2)}, u32[]{:S(2)}) collective-permute-start(bf16[64,16,128]{2,1,0:T(8,128)(2,1)S(1)} %fusion.7), channel_id=1, source_target_pairs={{0,1},{1,0},{2,3},{3,2},{4,5},{5,4},{6,7},{7,6},{8,9},{9,8},{10,11... | collective-permute-start | bytes 786440 | tf_op jit(solution)/shard_map/ppermute | solution.py:339

commit v3 on v1

--- a/solution.py
+++ b/solution.py
@@ -320,7 +320,7 @@
 
 def sent_over_x(parts):
     got = [parts[0]]
-    for shift in (2, 1, 3):
+    for shift in (1, 3, 2):
         route = [(x * 2 + y, (x + shift) % 4 * 2 + y) for x in range(4) for y in range(2)]
         got.append(lax.ppermute(parts[shift], "tm", route))
     return got

time: 240 us -> 241 us (level)
  waiting for transfers between devices: 122 us -> 125 us
    ppermute x6, starting transfers between devices: 10.6 us -> 8.14 us  [sent_over_x(): got.append(lax.ppermute(parts[shift], 'tm', route))]
where the time goes in v3:
time: 241 us; the launch traced here: 240 us
  waiting for transfers between devices  125 us (52%)
  Pallas kernels  51.4 us (21%)
  starting transfers between devices  45.4 us (19%)
  local copies, waits for them, and re-layouts  13.5 us (6%)
  other arithmetic  5.04 us (2%)
    all_to_all x5, waiting for transfers between devices, over_chan(): lax.all_to_all(blocks, 'chan', split_axis=0, concat_axis=0, tiled=True)  119 us
    all_to_all x5, starting transfers between devices, over_chan(): lax.all_to_all(blocks, 'chan', split_axis=0, concat_axis=0, tiled=True)  31.5 us
    pallas_call x2, Pallas kernels, correlate(): pl.pallas_call(functools.partial(correlate_kernel, steps), grid=(steps +...  26.7 us
    pallas_call x2, Pallas kernels, pick(): pl.pallas_call(pick_kernel, grid_spec=pltpu.PrefetchScalarGridSpec(num_sc...  9.05 us
    pallas_call x1, Pallas kernels, whiten(): pl.pallas_call(whiten_kernel, out_shape=jax.ShapeDtypeStruct((GROUPS, ROW...  8.63 us
    ppermute x6, starting transfers between devices, sent_over_x(): got.append(lax.ppermute(parts[shift], 'tm', route))  8.14 us
    unnamed x12, local copies, waits for them, and re-layouts  7.93 us
    pallas_call x1, Pallas kernels, expand(): pl.pallas_call(expand_kernel, grid=(GROUPS // per,), out_shape=jax.ShapeD...  7.11 us
  transfers between devices with their start and end apart: 14, of which 8 were waited for; matrix products, arithmetic and copies ran while one was open for 3% of the time, Pallas kernels for 16%

profile of v3, /device:TPU:1, one launch (start us, length us, event | category | flops | bytes accessed | tf_op | source)
XLA Modules:
  0.0 240.2 jit_solution(9121382374308093318)
XLA Ops:
  0.0 8.6 %whiten.1.spec = bf16[64,256,128]{2,1,0:T(8,128)(2,1)} custom-call(bf16[128,32,512]{2,1,0:T(8,128)(2,1)} %traces.1, f32[1,512]{1,0:T(1,128)} %constant.78.clone.taper_hbm, bf16[512,512]{1,0:T(8,128)(2,1)} %constant.79.clone.table_hbm), custom_call_target="tpu_custom_call" | custom-call | flops 2147483648 | bytes 8388608 | tf_op jit(solution)/shard_map/whiten/pallas_call | solution.py:123
  8.6 7.9 %all-to-all-start = ((bf16[16,1024,128]{2,1,0:T(8,128)(2,1)}), bf16[16,1024,128]{2,1,0:T(8,128)(2,1)}, u32[]{:S(2)}, u32[]{:S(2)}) async-start(bf16[16,1024,128]{2,1,0:T(8,128)(2,1)} %bitcast.57), calls=%async_computation | async-start | bytes 8388608 | tf_op jit(solution)/shard_map/all_to_all | solution.py:318
  17.8 2.2 copy-done
  20.0 7.1 %expand.1.own_hbm = bf16[64,512,256]{2,1,0:T(8,128)(2,1)S(1)} custom-call(bf16[64,256,128]{2,1,0:T(8,128)(2,1)S(1)} %copy-done), custom_call_target="tpu_custom_call" | custom-call | flops 67108864 | bytes 20971520 | tf_op jit(solution)/shard_map/expand/pallas_call | solution.py:158
  27.1 5.7 %copy-done.1 = bf16[64,512,256]{2,1,0:T(8,128)(2,1)} copy-done((bf16[64,512,256]{2,1,0:T(8,128)(2,1)}, bf16[64,512,256]{2,1,0:T(8,128)(2,1)S(1)}, u32[]{:S(2)}) %copy-start.1) | copy-done | bytes 16777240
  34.3 31.9 %all-to-all-done.source = bf16[16,1024,128]{2,1,0:T(8,128)(2,1)} async-done(((bf16[16,1024,128]{2,1,0:T(8,128)(2,1)}), bf16[16,1024,128]{2,1,0:T(8,128)(2,1)}, u32[]{:S(2)}, u32[]{:S(2)}) %all-to-all-start) | async-done | bytes 4194336 | tf_op jit(solution)/shard_map/all_to_all | solution.py:318
  66.2 4.5 %pick.2 = bf16[16,1024,128]{2,1,0:T(8,128)(2,1)} custom-call(s32[16]{0:T(128)} %fusion.10.index, bf16[16,1024,128]{2,1,0:T(8,128)(2,1)} %all-to-all-done.source), custom_call_target="tpu_custom_call" | custom-call | bytes 8388608 | tf_op jit(solution)/shard_map/pick/pallas_call | solution.py:279
  70.7 5.1 %all-to-all-start.1 = ((bf16[16,1024,128]{2,1,0:T(8,128)(2,1)}), bf16[16,1024,128]{2,1,0:T(8,128)(2,1)}, u32[]{:S(2)}, u32[]{:S(2)}) async-start(bf16[16,1024,128]{2,1,0:T(8,128)(2,1)} %pick.2), calls=%async_computation.1 | async-start | bytes 8388608 | tf_op jit(solution)/shard_map/all_to_all | solution.py:318
  75.9 4.5 %pick.3 = bf16[16,1024,128]{2,1,0:T(8,128)(2,1)} custom-call(s32[16]{0:T(128)} %get-tuple-element.65.index, bf16[16,1024,128]{2,1,0:T(8,128)(2,1)} %all-to-all-done.source), custom_call_target="tpu_custom_call" | custom-call | bytes 8388608 | tf_op jit(solution)/shard_map/pick/pallas_call | solution.py:279
  80.4 45.2 %all-to-all-done.1 = bf16[16,1024,128]{2,1,0:T(8,128)(2,1)} async-done(((bf16[16,1024,128]{2,1,0:T(8,128)(2,1)}), bf16[16,1024,128]{2,1,0:T(8,128)(2,1)}, u32[]{:S(2)}, u32[]{:S(2)}) %all-to-all-start.1) | async-done | bytes 4194336 | tf_op jit(solution)/shard_map/all_to_all | solution.py:318
  125.6 5.2 %all-to-all-start.2 = ((bf16[16,1024,128]{2,1,0:T(8,128)(2,1)}), bf16[16,1024,128]{2,1,0:T(8,128)(2,1)}, u32[]{:S(2)}, u32[]{:S(2)}) async-start(bf16[16,1024,128]{2,1,0:T(8,128)(2,1)} %pick.3), calls=%async_computation.2 | async-start | bytes 8388608 | tf_op jit(solution)/shard_map/all_to_all | solution.py:318
  131.4 13.4 %correlate_both.1 = (bf16[2,2,64,16,128]{4,3,2,1,0:T(8,128)(2,1)}, bf16[2,2,64,16,128]{4,3,2,1,0:T(8,128)(2,1)}, bf16[2,2,64,16,128]{4,3,2,1,0:T(8,128)(2,1)}, bf16[2,2,64,16,128]{4,3,2,1,0:T(8,128)(2,1)}) custom-call(bf16[64,512,256]{2,1,0:T(8,128)(2,1)} %copy-done.1, bf16[64,256,128]{2,1,0:T(8,128)(2,1)} %bitcast.4.partner_hbm, ...), custom_call_target="tpu_custom_call" | custom-call | flops 17179869184 | bytes 25165824 | tf_op jit(solution)/shard_map/correlate_both/pallas_call | solution.py:240
  147.6 1.5 collective-permute-start.2
  149.1 31.5 %all-to-all-done.2 = bf16[16,1024,128]{2,1,0:T(8,128)(2,1)} async-done(((bf16[16,1024,128]{2,1,0:T(8,128)(2,1)}), bf16[16,1024,128]{2,1,0:T(8,128)(2,1)}, u32[]{:S(2)}, u32[]{:S(2)}) %all-to-all-start.2) | async-done | bytes 4194336 | tf_op jit(solution)/shard_map/all_to_all | solution.py:318
  180.6 13.2 %correlate_one.1 = (bf16[2,1,64,16,128]{4,3,2,1,0:T(8,128)(2,1)}, bf16[2,1,64,16,128]{4,3,2,1,0:T(8,128)(2,1)}, bf16[2,1,64,16,128]{4,3,2,1,0:T(8,128)(2,1)}, bf16[2,1,64,16,128]{4,3,2,1,0:T(8,128)(2,1)}) custom-call(bf16[64,512,256]{2,1,0:T(8,128)(2,1)} %copy-done.1, bf16[64,256,128]{2,1,0:T(8,128)(2,1)} %bitcast.6.partner_hbm, ...), custom_call_target="tpu_custom_call" | custom-call | flops 17179869184 | bytes 25165824 | tf_op jit(solution)/shard_map/correlate_one/pallas_call | solution.py:240
  194.9 2.7 %collective-permute-start.4 = (bf16[64,16,128]{2,1,0:T(8,128)(2,1)S(1)}, bf16[64,16,128]{2,1,0:T(8,128)(2,1)S(1)}, u32[]{:S(2)}, u32[]{:S(2)}) collective-permute-start(bf16[64,16,128]{2,1,0:T(8,128)(2,1)S(1)} %fusion.6), channel_id=1, source_target_pairs={{0,1},{1,0},{2,3},{3,2},{4,5},{5,4},{6,7},{7,6},{8,9},{9,8},{10,11... | collective-permute-start | bytes 786440 | tf_op jit(solution)/shard_map/ppermute | solution.py:339
  198.9 1.8 collective-permute-start.6
  203.9 9.2 %all-to-all-start.3 = ((bf16[16,64,128]{2,1,0:T(8,128)(2,1)}), bf16[16,64,128]{2,1,0:T(8,128)(2,1)S(1)}, u32[]{:S(2)}, u32[]{:S(2)}) async-start(bf16[16,64,128]{2,1,0:T(8,128)(2,1)} %bitcast.13), calls=%async_computation.3 | async-start | bytes 524288 | tf_op jit(solution)/shard_map/all_to_all | solution.py:318
  213.5 7.0 %all-to-all-done.3 = bf16[16,64,128]{2,1,0:T(8,128)(2,1)S(1)} async-done(((bf16[16,64,128]{2,1,0:T(8,128)(2,1)}), bf16[16,64,128]{2,1,0:T(8,128)(2,1)S(1)}, u32[]{:S(2)}, u32[]{:S(2)}) %all-to-all-start.3) | async-done | bytes 262176 | tf_op jit(solution)/shard_map/all_to_all | solution.py:318
  221.8 4.1 %all-to-all-start.4 = ((bf16[16,64,128]{2,1,0:T(8,128)(2,1)}), bf16[16,64,128]{2,1,0:T(8,128)(2,1)S(1)}, u32[]{:S(2)}, u32[]{:S(2)}) async-start(bf16[16,64,128]{2,1,0:T(8,128)(2,1)} %gather_fusion), calls=%async_computation.4 | async-start | bytes 524288 | tf_op jit(solution)/shard_map/all_to_all | solution.py:318
  227.4 2.7 %collective-permute-start.8 = (bf16[64,16,128]{2,1,0:T(8,128)(2,1)S(1)}, bf16[64,16,128]{2,1,0:T(8,128)(2,1)S(1)}, u32[]{:S(2)}, u32[]{:S(2)}) collective-permute-start(bf16[64,16,128]{2,1,0:T(8,128)(2,1)S(1)} %fusion.7), channel_id=1, source_target_pairs={{0,1},{1,0},{2,3},{3,2},{4,5},{5,4},{6,7},{7,6},{8,9},{9,8},{10,11... | collective-permute-start | bytes 786440 | tf_op jit(solution)/shard_map/ppermute | solution.py:339
  230.1 3.1 %all-to-all-done.4 = bf16[16,64,128]{2,1,0:T(8,128)(2,1)S(1)} async-done(((bf16[16,64,128]{2,1,0:T(8,128)(2,1)}), bf16[16,64,128]{2,1,0:T(8,128)(2,1)S(1)}, u32[]{:S(2)}, u32[]{:S(2)}) %all-to-all-start.4) | async-done | bytes 262176 | tf_op jit(solution)/shard_map/all_to_all | solution.py:318
  234.0 4.1 %collective-permute-done.8 = bf16[64,16,128]{2,1,0:T(8,128)(2,1)S(1)} collective-permute-done((bf16[64,16,128]{2,1,0:T(8,128)(2,1)S(1)}, bf16[64,16,128]{2,1,0:T(8,128)(2,1)S(1)}, u32[]{:S(2)}, u32[]{:S(2)}) %collective-permute-start.8) | collective-permute-done | bytes 262176 | tf_op jit(solution)/shard_map/ppermute | solution.py:339
  238.5 1.7 copy.13
  (52 shorter events, 15.8 us)
Async XLA Ops:
  8.6 7.9 %copy-start.5 = (s32[3,16]{1,0:T(4,128)S(1)}, s32[3,16]{1,0:T(4,128)}, u32[]{:S(2)}) copy-start(s32[3,16]{1,0:T(4,128)} %param.6) | copy-start | bytes 580
  8.6 57.5 %all-to-all-start = ((bf16[16,1024,128]{2,1,0:T(8,128)(2,1)}), bf16[16,1024,128]{2,1,0:T(8,128)(2,1)}, u32[]{:S(2)}, u32[]{:S(2)}) async-start(bf16[16,1024,128]{2,1,0:T(8,128)(2,1)} %bitcast.57), calls=%async_computation | async-start | bytes 8388608 | tf_op jit(solution)/shard_map/all_to_all | solution.py:318
  17.8 2.2 copy-start
  20.0 13.0 %copy-start.4 = (bf16[2,256,512]{2,1,0:T(8,128)(2,1)S(1)}, bf16[2,256,512]{2,1,0:T(8,128)(2,1)}, u32[]{:S(2)}) copy-start(bf16[2,256,512]{2,1,0:T(8,128)(2,1)} %constant.80.clone) | copy-start | bytes 1572868
  27.1 5.7 %copy-start.1 = (bf16[64,512,256]{2,1,0:T(8,128)(2,1)}, bf16[64,512,256]{2,1,0:T(8,128)(2,1)S(1)}, u32[]{:S(2)}) copy-start(bf16[64,512,256]{2,1,0:T(8,128)(2,1)S(1)} %expand.1.own_hbm) | copy-start | bytes 50331652
  70.7 54.9 %all-to-all-start.1 = ((bf16[16,1024,128]{2,1,0:T(8,128)(2,1)}), bf16[16,1024,128]{2,1,0:T(8,128)(2,1)}, u32[]{:S(2)}, u32[]{:S(2)}) async-start(bf16[16,1024,128]{2,1,0:T(8,128)(2,1)} %pick.2), calls=%async_computation.1 | async-start | bytes 8388608 | tf_op jit(solution)/shard_map/all_to_all | solution.py:318
  125.6 54.9 %all-to-all-start.2 = ((bf16[16,1024,128]{2,1,0:T(8,128)(2,1)}), bf16[16,1024,128]{2,1,0:T(8,128)(2,1)}, u32[]{:S(2)}, u32[]{:S(2)}) async-start(bf16[16,1024,128]{2,1,0:T(8,128)(2,1)} %pick.3), calls=%async_computation.2 | async-start | bytes 8388608 | tf_op jit(solution)/shard_map/all_to_all | solution.py:318
  144.8 49.0 %collective-permute-start = (bf16[2,2,64,16,128]{4,3,2,1,0:T(8,128)(2,1)}, bf16[2,2,64,16,128]{4,3,2,1,0:T(8,128)(2,1)S(1)}, u32[]{:S(2)}, u32[]{:S(2)}) collective-permute-start(bf16[2,2,64,16,128]{4,3,2,1,0:T(8,128)(2,1)} %get-tuple-element.35), channel_id=1, source_target_pairs={{0,2},{1,3},{2,4},{3,5},{4,6},{5,7},{6,0},{7,1},{8,10},{9,11},{10,... | collective-permute-start | bytes 3145736 | tf_op jit(solution)/shard_map/ppermute | solution.py:325
  146.1 47.7 %collective-permute-start.1 = (bf16[2,2,64,16,128]{4,3,2,1,0:T(8,128)(2,1)}, bf16[2,2,64,16,128]{4,3,2,1,0:T(8,128)(2,1)S(1)}, u32[]{:S(2)}, u32[]{:S(2)}) collective-permute-start(bf16[2,2,64,16,128]{4,3,2,1,0:T(8,128)(2,1)} %get-tuple-element.36), channel_id=1, source_target_pairs={{0,6},{1,7},{2,0},{3,1},{4,2},{5,3},{6,4},{7,5},{8,14},{9,15},{10,... | collective-permute-start | bytes 3145736 | tf_op jit(solution)/shard_map/ppermute | solution.py:325
  147.6 46.6 %collective-permute-start.2 = (bf16[2,2,64,16,128]{4,3,2,1,0:T(8,128)(2,1)}, bf16[2,2,64,16,128]{4,3,2,1,0:T(8,128)(2,1)S(1)}, u32[]{:S(2)}, u32[]{:S(2)}) collective-permute-start(bf16[2,2,64,16,128]{4,3,2,1,0:T(8,128)(2,1)} %get-tuple-element.37), channel_id=1, source_target_pairs={{0,4},{1,5},{2,6},{3,7},{4,0},{5,1},{6,2},{7,3},{8,12},{9,13},{10,... | collective-permute-start | bytes 3145736 | tf_op jit(solution)/shard_map/ppermute | solution.py:325
  180.6 13.6 %copy-start.2 = (bf16[2,2,64,16,128]{4,3,2,1,0:T(8,128)(2,1)S(1)}, bf16[2,2,64,16,128]{4,3,2,1,0:T(8,128)(2,1)}, u32[]{:S(2)}) copy-start(bf16[2,2,64,16,128]{4,3,2,1,0:T(8,128)(2,1)} %get-tuple-element.42) | copy-start | bytes 3145732
  194.9 8.3 %collective-permute-start.4 = (bf16[64,16,128]{2,1,0:T(8,128)(2,1)S(1)}, bf16[64,16,128]{2,1,0:T(8,128)(2,1)S(1)}, u32[]{:S(2)}, u32[]{:S(2)}) collective-permute-start(bf16[64,16,128]{2,1,0:T(8,128)(2,1)S(1)} %fusion.6), channel_id=1, source_target_pairs={{0,1},{1,0},{2,3},{3,2},{4,5},{5,4},{6,7},{7,6},{8,9},{9,8},{10,11... | collective-permute-start | bytes 786440 | tf_op jit(solution)/shard_map/ppermute | solution.py:339
  197.6 15.5 %collective-permute-start.3 = (bf16[64,16,128]{2,1,0:T(8,128)(2,1)S(1)}, bf16[64,16,128]{2,1,0:T(8,128)(2,1)S(1)}, u32[]{:S(2)}, u32[]{:S(2)}) collective-permute-start(bf16[64,16,128]{2,1,0:T(8,128)(2,1)S(1)} %fusion.5), channel_id=1, source_target_pairs={{0,1},{1,0},{2,3},{3,2},{4,5},{5,4},{6,7},{7,6},{8,9},{9,8},{10,11... | collective-permute-start | bytes 786440 | tf_op jit(solution)/shard_map/ppermute | solution.py:339
  198.1 27.8 %collective-permute-start.5 = (bf16[2,1,64,16,128]{4,3,2,1,0:T(8,128)(2,1)}, bf16[2,1,64,16,128]{4,3,2,1,0:T(8,128)(2,1)S(1)}, u32[]{:S(2)}, u32[]{:S(2)}) collective-permute-start(bf16[2,1,64,16,128]{4,3,2,1,0:T(8,128)(2,1)} %get-tuple-element.48), channel_id=1, source_target_pairs={{0,2},{1,3},{2,4},{3,5},{4,6},{5,7},{6,0},{7,1},{8,10},{9,11},{10,... | collective-permute-start | bytes 1572872 | tf_op jit(solution)/shard_map/ppermute | solution.py:325
  198.9 27.0 %collective-permute-start.6 = (bf16[2,1,64,16,128]{4,3,2,1,0:T(8,128)(2,1)}, bf16[2,1,64,16,128]{4,3,2,1,0:T(8,128)(2,1)}, u32[]{:S(2)}, u32[]{:S(2)}) collective-permute-start(bf16[2,1,64,16,128]{4,3,2,1,0:T(8,128)(2,1)} %get-tuple-element.49), channel_id=1, source_target_pairs={{0,6},{1,7},{2,0},{3,1},{4,2},{5,3},{6,4},{7,5},{8,14},{9,15},{10,... | collective-permute-start | bytes 1572872 | tf_op jit(solution)/shard_map/ppermute | solution.py:325
  200.7 25.2 %collective-permute-start.7 = (bf16[2,1,64,16,128]{4,3,2,1,0:T(8,128)(2,1)}, bf16[2,1,64,16,128]{4,3,2,1,0:T(8,128)(2,1)}, u32[]{:S(2)}, u32[]{:S(2)}) collective-permute-start(bf16[2,1,64,16,128]{4,3,2,1,0:T(8,128)(2,1)} %get-tuple-element.50), channel_id=1, source_target_pairs={{0,4},{1,5},{2,6},{3,7},{4,0},{5,1},{6,2},{7,3},{8,12},{9,13},{10,... | collective-permute-start | bytes 1572872 | tf_op jit(solution)/shard_map/ppermute | solution.py:325
  203.9 22.0 %copy-start.3 = (bf16[2,1,64,16,128]{4,3,2,1,0:T(8,128)(2,1)S(1)}, bf16[2,1,64,16,128]{4,3,2,1,0:T(8,128)(2,1)}, u32[]{:S(2)}) copy-start(bf16[2,1,64,16,128]{4,3,2,1,0:T(8,128)(2,1)} %get-tuple-element.51) | copy-start | bytes 1572868
  203.9 16.6 %all-to-all-start.3 = ((bf16[16,64,128]{2,1,0:T(8,128)(2,1)}), bf16[16,64,128]{2,1,0:T(8,128)(2,1)S(1)}, u32[]{:S(2)}, u32[]{:S(2)}) async-start(bf16[16,64,128]{2,1,0:T(8,128)(2,1)} %bitcast.13), calls=%async_computation.3 | async-start | bytes 524288 | tf_op jit(solution)/shard_map/all_to_all | solution.py:318
  221.8 11.4 %all-to-all-start.4 = ((bf16[16,64,128]{2,1,0:T(8,128)(2,1)}), bf16[16,64,128]{2,1,0:T(8,128)(2,1)S(1)}, u32[]{:S(2)}, u32[]{:S(2)}) async-start(bf16[16,64,128]{2,1,0:T(8,128)(2,1)} %gather_fusion), calls=%async_computation.4 | async-start | bytes 524288 | tf_op jit(solution)/shard_map/all_to_all | solution.py:318
  227.4 10.7 %collective-permute-start.8 = (bf16[64,16,128]{2,1,0:T(8,128)(2,1)S(1)}, bf16[64,16,128]{2,1,0:T(8,128)(2,1)S(1)}, u32[]{:S(2)}, u32[]{:S(2)}) collective-permute-start(bf16[64,16,128]{2,1,0:T(8,128)(2,1)S(1)} %fusion.7), channel_id=1, source_target_pairs={{0,1},{1,0},{2,3},{3,2},{4,5},{5,4},{6,7},{7,6},{8,9},{9,8},{10,11... | collective-permute-start | bytes 786440 | tf_op jit(solution)/shard_map/ppermute | solution.py:339
